TPU v7x, 32 devices: a whole 2x2x4 slice. The times are simulated.
32 devices in a mesh: ctx: 8 (over y, x, core), exp: 4 (over z).
Axes of the slice: x: 2, y: 2, z: 4, core: 2. Of those that a mesh axis runs over, the one named last changes fastest.
Arguments:
- inputs: bfloat16 [1024, 1024], P('exp', 'ctx'), may hold values from -6 to 6
- conv_taps: float32 [1024, 31], P('exp'), may hold values from -1 to 1
- norm_gain: bfloat16 [1024], P('exp'), may hold values from 0.099609375 to 1.8984375
- routes: int32 [1024, 2], P('ctx'), may hold values from 0 to 7, all different within a row; in each aligned block of 128 rows (0 to 127, 128 to 255, ...) at most 32 rows name the same one
- gate_probs: float32 [1024, 2], P('ctx'), may hold values from 0.1 to 0.9
- w_gate: bfloat16 [8, 1024, 4096], P('ctx', None, 'exp'), may hold values from -0.1875 to 0.1875
- w_up: bfloat16 [8, 1024, 4096], P('ctx', None, 'exp'), may hold values from -0.1875 to 0.1875
- w_down: bfloat16 [8, 4096, 1024], P('ctx', 'exp'), may hold values from -0.09375 to 0.09375
- grad_out: bfloat16 [1024, 1024], P('exp', 'ctx'), may hold values from -6 to 6
Outputs:
- layer_out: bfloat16 [1024, 1024], P('exp', 'ctx')
- grad_inputs: bfloat16 [1024, 1024], P('exp', 'ctx')
- grad_taps: float32 [1024, 31], P('exp')
- grad_gain: float32 [1024], P('exp')
- grad_gates: float32 [1024, 2], P('ctx')
- grad_w_gate: bfloat16 [8, 1024, 4096], P('ctx', None, 'exp')
- grad_w_up: bfloat16 [8, 1024, 4096], P('ctx', None, 'exp')
- grad_w_down: bfloat16 [8, 4096, 1024], P('ctx', 'exp')
Inputs may be any that keep to these rules, and one draw needn't show every extreme that they name: `routes`: in each aligned block of 128 rows (the rows of one index of ctx) no expert is named by more than 32 rows, a bound that some block reaches; the two experts of a row differ.
All inputs are finite; a program needn't handle non-finite values.
Results may differ from a plain program's by a relative error of at most 0.025.
Values may be sent and summed in bfloat16 or wider, within the bound.
A program may use at most 64 MiB of HBM per device.

v0:
```python
import functools
import jax
import jax.numpy as jnp
from jax import lax
from jax.experimental import pallas as pl
from jax.experimental.pallas import tpu as pltpu
from jax.sharding import PartitionSpec as P

EPS = 1e-05
MESH = pl.DeviceIdType.MESH
F32, BF16 = jnp.float32, jnp.bfloat16
LAST = (((1,), (1,)), ((), ()))
FIRST = (((0,), (0,)), ((), ()))


def greet(n, m):
    c, e = lax.axis_index("ctx"), lax.axis_index("exp")
    barrier = pltpu.get_barrier_semaphore()

    def ctx_peer(k, _):
        pl.semaphore_signal(barrier, inc=1, device_id=(lax.rem(c + k, n), e), device_id_type=MESH)
        return 0

    def exp_peer(k, _):
        pl.semaphore_signal(barrier, inc=1, device_id=(c, lax.rem(e + k, m)), device_id_type=MESH)
        return 0

    lax.fori_loop(1, n, ctx_peer, 0)
    lax.fori_loop(1, m, exp_peer, 0)
    pl.semaphore_wait(barrier, n + m - 2)


class Exchange:
    def __init__(self, axis, size, src, dst, send, recv):
        self.axis, self.size, self.src, self.dst = axis, size, src, dst
        self.send, self.recv = send, recv
        self.me = lax.axis_index(axis)

    def to(self, k):
        peer = lax.rem(self.me + k, self.size)
        if self.axis == "ctx":
            where = (peer, lax.axis_index("exp"))
        else:
            where = (lax.axis_index("ctx"), peer)
        return pltpu.make_async_remote_copy(
            src_ref=self.src(peer),
            dst_ref=self.dst(self.me),
            send_sem=self.send.at[peer],
            recv_sem=self.recv.at[self.me],
            device_id=where,
            device_id_type=MESH,
        )

    def frm(self, k):
        peer = lax.rem(self.me + k, self.size)
        if self.axis == "ctx":
            where = (peer, lax.axis_index("exp"))
        else:
            where = (lax.axis_index("ctx"), peer)
        return pltpu.make_async_remote_copy(
            src_ref=self.src(peer),
            dst_ref=self.dst(peer),
            send_sem=self.send.at[peer],
            recv_sem=self.recv.at[peer],
            device_id=where,
            device_id_type=MESH,
        )

    def each(self, act):
        def body(k, _):
            act(k)
            return 0

        lax.fori_loop(1, self.size, body, 0)

    def start(self):
        self.each(lambda k: self.to(k).start())

    def arrive(self):
        self.each(lambda k: self.frm(k).wait_recv())

    def sent(self):
        self.each(lambda k: self.to(k).wait_send())


class Halo:
    def __init__(self, n, block, left, right, sems):
        c, e = lax.axis_index("ctx"), lax.axis_index("exp")
        up, down = lax.rem(c + 1, n), lax.rem(c + n - 1, n)
        make = pltpu.make_async_remote_copy
        self.copies = [
            make(block, left, sems.at[0], sems.at[1], device_id=(up, e), device_id_type=MESH),
            make(block, right, sems.at[2], sems.at[3], device_id=(down, e), device_id_type=MESH),
        ]

    def start(self):
        for copy in self.copies:
            copy.start()

    def arrive(self):
        for copy in self.copies:
            copy.wait_recv()

    def sent(self):
        for copy in self.copies:
            copy.wait_send()


def shifted(block, left, right, offset, lane):
    width = block.shape[1]
    if offset == 0:
        return block
    if offset > 0:
        return pltpu.roll(jnp.where(lane >= offset, block, right), width - offset, axis=1)
    return pltpu.roll(jnp.where(lane < width + offset, block, left), -offset, axis=1)


def picks(aux, capacity, slots):
    tokens = aux.shape[0]
    lanes = lax.broadcasted_iota(jnp.int32, (tokens, 128), 1)
    named = [aux[:, k : k + 1].astype(jnp.int32) for k in range(2)]
    hot = [(lanes == r).astype(F32) for r in named]
    row = lax.broadcasted_iota(jnp.int32, (tokens, tokens), 0)
    col = lax.broadcasted_iota(jnp.int32, (tokens, tokens), 1)
    earlier = (col < row).astype(F32).astype(BF16)
    count = jnp.dot(earlier, (hot[0] + hot[1]).astype(BF16), preferred_element_type=F32)
    place = lax.broadcasted_iota(jnp.int32, (tokens, slots), 1)
    out = []
    for r, h in zip(named, hot):
        slot = jnp.sum(count * h, axis=1, keepdims=True).astype(jnp.int32)
        out.append((place == r * capacity + slot).astype(F32))
    return out


def front(n, m, taps, capacity, x_ref, pack_ref, aux_ref, cot_ref,
          rx_ref, rdy_ref, mixed_ref, scale_ref, left_ref, right_ref, cots_ref,
          nrm, sq, sx, sdy, hs, cs, cr, qs, qr, ns, nr, ys, yr, xs, xr):
    me, mine = lax.axis_index("ctx"), lax.axis_index("exp")
    chans, tokens = x_ref.shape
    slots, width = sx.shape
    half = taps // 2
    greet(n, m)
    halo = Halo(n, x_ref, left_ref, right_ref, hs)
    halo.start()
    gather_cot = Exchange("exp", m, lambda p: cot_ref, lambda s: cots_ref.at[s], cs, cr)
    gather_cot.start()
    cots_ref[mine] = cot_ref[...]
    aux = aux_ref[...]
    p0, p1 = picks(aux, capacity, slots)
    pt = jnp.transpose(p0 + p1).astype(BF16)
    gated = jnp.transpose(p0 * aux[:, 2:3] + p1 * aux[:, 3:4])
    gate = jnp.sum(gated, axis=1, keepdims=True)

    halo.arrive()
    x = x_ref[...].astype(F32)
    left, right = left_ref[...].astype(F32), right_ref[...].astype(F32)
    pack = pack_ref[...]
    lane = lax.broadcasted_iota(jnp.int32, (chans, tokens), 1)
    conv = jnp.zeros((chans, tokens), F32)
    for j in range(taps):
        conv = conv + pack[:, j : j + 1] * shifted(x, left, right, j - half, lane)
    mixed = (x + conv).astype(BF16)
    mixed_ref[...] = mixed
    mixed = mixed.astype(F32)
    sq[mine] = jnp.broadcast_to(jnp.sum(mixed * mixed, axis=0, keepdims=True), (8, tokens))
    squares = Exchange("exp", m, lambda p: sq.at[mine], lambda s: sq.at[s], qs, qr)
    squares.start()

    def rows(ref):
        return lambda p: ref.at[pl.ds(pl.multiple_of(p * capacity, capacity), capacity)]

    own = pl.ds(pl.multiple_of(me * capacity, capacity), capacity)
    gather_cot.arrive()
    for k in range(m):
        part = lax.dot_general(pt, cots_ref[k], LAST, preferred_element_type=F32)
        sdy[:, k * chans : (k + 1) * chans] = (part * gate).astype(BF16)
    send_dy = Exchange("ctx", n, rows(sdy), rows(rdy_ref), ys, yr)
    squares.arrive()
    total = jnp.sum(sq[...], axis=0)
    scale = lax.rsqrt(total / width + EPS)
    scale_ref[...] = scale
    nrm[mine] = (mixed * pack[:, taps : taps + 1] * scale[:1]).astype(BF16)
    gather_x = Exchange("exp", m, lambda p: nrm.at[mine], lambda s: nrm.at[s], ns, nr)
    gather_x.start()
    send_dy.start()
    rdy_ref[own, :] = sdy[own, :]
    gather_x.arrive()
    for k in range(m):
        part = lax.dot_general(pt, nrm[k], LAST, preferred_element_type=F32)
        sx[:, k * chans : (k + 1) * chans] = part.astype(BF16)
    send_x = Exchange("ctx", n, rows(sx), rows(rx_ref), xs, xr)
    send_x.start()
    rx_ref[own, :] = sx[own, :]
    send_dy.arrive()
    send_x.arrive()
    for done in (halo, gather_cot, squares, send_dy, gather_x, send_x):
        done.sent()


def back(n, m, taps, capacity, y_ref, dx_ref, x_ref, left_ref, right_ref, pack_ref, aux_ref, cot_ref,
         cots_ref, mixed_ref, scale_ref,
         out_ref, gin_ref, tap_ref, gg_ref,
         by, bdx, zdx, zy, rdx, ry, dots, norm, dm, dl, dr, tp,
         ds_, dr_, ys, yr, as_, ar, bs, br, gs, gr, qs, qr, hs, ts, tr):
    me, mine = lax.axis_index("ctx"), lax.axis_index("exp")
    chans, tokens = x_ref.shape
    slots, width = by.shape
    half = taps // 2
    greet(n, m)

    def rows(ref):
        return lambda p: ref.at[pl.ds(pl.multiple_of(p * capacity, capacity), capacity)]

    own = pl.ds(pl.multiple_of(me * capacity, capacity), capacity)
    send_dx = Exchange("ctx", n, rows(dx_ref), rows(bdx), ds_, dr_)
    send_y = Exchange("ctx", n, rows(y_ref), rows(by), ys, yr)
    send_dx.start()
    send_y.start()
    bdx[own, :] = dx_ref[own, :]
    by[own, :] = y_ref[own, :]
    aux = aux_ref[...]
    p0, p1 = picks(aux, capacity, slots)
    both = (p0 + p1).astype(BF16)
    p0, p1 = p0.astype(BF16), p1.astype(BF16)
    x = x_ref[...].astype(F32)
    left, right = left_ref[...].astype(F32), right_ref[...].astype(F32)
    mixed = mixed_ref[...].astype(F32)
    pack = pack_ref[...]
    gain = pack[:, taps : taps + 1]
    scale = scale_ref[:1]
    cot = cot_ref[...].astype(F32)

    send_dx.arrive()
    for k in range(m):
        part = jnp.dot(both, bdx[:, k * chans : (k + 1) * chans], preferred_element_type=F32)
        zdx[k] = part.astype(BF16)
    sum_dx = Exchange("exp", m, lambda p: zdx.at[p], lambda s: rdx.at[s], as_, ar)
    sum_dx.start()
    rdx[mine] = zdx[mine]
    send_y.arrive()
    d0 = jnp.zeros((tokens, 1), F32)
    d1 = jnp.zeros((tokens, 1), F32)
    for k in range(m):
        block = by[:, k * chans : (k + 1) * chans]
        y0 = jnp.dot(p0, block, preferred_element_type=F32)
        y1 = jnp.dot(p1, block, preferred_element_type=F32)
        zy[k] = (y0 * aux[:, 2:3] + y1 * aux[:, 3:4]).astype(BF16)
        turned = jnp.transpose(cots_ref[k].astype(F32))
        d0 = d0 + jnp.sum(y0 * turned, axis=1, keepdims=True)
        d1 = d1 + jnp.sum(y1 * turned, axis=1, keepdims=True)
    sum_y = Exchange("exp", m, lambda p: zy.at[p], lambda s: ry.at[s], bs, br)
    sum_y.start()
    ry[mine] = zy[mine]
    col = lax.broadcasted_iota(jnp.int32, (tokens, 128), 1)
    dots[mine] = jnp.transpose(jnp.where(col == 0, d0, jnp.where(col == 1, d1, 0.0)))[:8]
    sum_dots = Exchange("exp", m, lambda p: dots.at[mine], lambda s: dots.at[s], gs, gr)
    sum_dots.start()

    sum_dx.arrive()
    dn = jnp.transpose(jnp.sum(rdx[...].astype(F32), axis=0))
    weighted = dn * mixed
    norm[mine] = jnp.broadcast_to(jnp.sum(weighted * gain, axis=0, keepdims=True), (8, tokens))
    sum_norm = Exchange("exp", m, lambda p: norm.at[mine], lambda s: norm.at[s], qs, qr)
    sum_norm.start()
    lane = lax.broadcasted_iota(jnp.int32, (chans, tokens), 1)
    gain_grad = jnp.sum(weighted * scale, axis=1, keepdims=True)
    sum_norm.arrive()
    q = jnp.sum(norm[...], axis=0)[:1]
    d_mixed = cot + gain * dn * scale - mixed * (q * scale * scale * scale / width)
    dm[...] = d_mixed.astype(BF16)
    halo = Halo(n, dm, dl, dr, hs)
    halo.start()
    grads = jnp.where(lane == taps, gain_grad, 0.0)
    for j in range(taps):
        term = jnp.sum(d_mixed * shifted(x, left, right, j - half, lane), axis=1, keepdims=True)
        grads = jnp.where(lane == j, term, grads)
    tp[me] = jnp.transpose(grads)[: tp.shape[1]]
    sum_taps = Exchange("ctx", n, lambda p: tp.at[me], lambda s: tp.at[s], ts, tr)
    sum_taps.start()
    halo.arrive()
    dleft, dright = dl[...].astype(F32), dr[...].astype(F32)
    grad = d_mixed
    for j in range(taps):
        grad = grad + pack[:, j : j + 1] * shifted(d_mixed, dleft, dright, half - j, lane)
    gin_ref[...] = grad.astype(BF16)
    sum_y.arrive()
    out_ref[...] = (mixed + jnp.transpose(jnp.sum(ry[...].astype(F32), axis=0))).astype(BF16)
    sum_dots.arrive()
    gg_ref[...] = jnp.sum(dots[...], axis=0)
    sum_taps.arrive()
    tap_ref[...] = jnp.sum(tp[...], axis=0)
    for done in (send_dx, send_y, sum_dx, sum_y, sum_dots, sum_norm, halo, sum_taps):
        done.sent()


def sems(*counts):
    out = []
    for count in counts:
        out += [pltpu.SemaphoreType.DMA((count,)), pltpu.SemaphoreType.DMA((count,))]
    return out


def local(inputs, conv_taps, norm_gain, routes, gate_probs, w_gate, w_up, w_down, grad_out):
    chans, tokens = inputs.shape
    taps = conv_taps.shape[1]
    width = w_gate.shape[1]
    n, m = lax.axis_size("ctx"), lax.axis_size("exp")
    capacity = max(tokens // 8, (2 * tokens + n - 1) // n)
    slots = n * capacity
    pad = -(-(taps + 1) // 8) * 8
    pack = jnp.concatenate([conv_taps, norm_gain.astype(F32)[:, None]], axis=1)
    aux = jnp.concatenate([routes.astype(F32), gate_probs], axis=1)
    vmem = pl.BlockSpec(memory_space=pltpu.VMEM)
    shape = jax.ShapeDtypeStruct
    rx, rdy, mixed, scale, left, right, cots = pl.pallas_call(
        functools.partial(front, n, m, taps, capacity),
        out_shape=(
            shape((slots, width), BF16),
            shape((slots, width), BF16),
            shape((chans, tokens), BF16),
            shape((8, tokens), F32),
            shape((chans, tokens), BF16),
            shape((chans, tokens), BF16),
            shape((m, chans, tokens), BF16),
        ),
        in_specs=[vmem] * 4,
        out_specs=(vmem,) * 7,
        scratch_shapes=[
            pltpu.VMEM((m, chans, tokens), BF16),
            pltpu.VMEM((m, 8, tokens), F32),
            pltpu.VMEM((slots, width), BF16),
            pltpu.VMEM((slots, width), BF16),
            pltpu.SemaphoreType.DMA((4,)),
            *sems(m, m, m, n, n),
        ],
        compiler_params=pltpu.CompilerParams(
            collective_id=0, has_side_effects=True, vmem_limit_bytes=40 << 20
        ),
        name="front",
    )(inputs, pack, aux, grad_out)
    weight_gate, weight_up, weight_down = w_gate[0], w_up[0], w_down[0]
    gate_act = jnp.dot(rx, weight_gate, preferred_element_type=F32)
    up_act = jnp.dot(rx, weight_up, preferred_element_type=F32)
    sigma = jax.nn.sigmoid(gate_act)
    hidden = (gate_act * sigma * up_act).astype(BF16)
    result = jnp.dot(hidden, weight_down, preferred_element_type=F32).astype(BF16)
    d_hidden = lax.dot_general(rdy, weight_down, LAST, preferred_element_type=F32)
    d_gate = (d_hidden * up_act * sigma * (1.0 + gate_act * (1.0 - sigma))).astype(BF16)
    d_up = (d_hidden * gate_act * sigma).astype(BF16)
    d_rows = lax.dot_general(d_gate, weight_gate, LAST, preferred_element_type=F32)
    d_rows = d_rows + lax.dot_general(d_up, weight_up, LAST, preferred_element_type=F32)
    d_rows = d_rows.astype(BF16)
    grad_down = lax.dot_general(hidden, rdy, FIRST, preferred_element_type=F32).astype(BF16)
    grad_gate = lax.dot_general(rx, d_gate, FIRST, preferred_element_type=F32).astype(BF16)
    grad_up = lax.dot_general(rx, d_up, FIRST, preferred_element_type=F32).astype(BF16)
    layer_out, grad_in, tap_sum, gate_sum = pl.pallas_call(
        functools.partial(back, n, m, taps, capacity),
        out_shape=(
            shape((chans, tokens), BF16),
            shape((chans, tokens), BF16),
            shape((pad, chans), F32),
            shape((8, tokens), F32),
        ),
        in_specs=[vmem] * 11,
        out_specs=(vmem,) * 4,
        scratch_shapes=[
            pltpu.VMEM((slots, width), BF16),
            pltpu.VMEM((slots, width), BF16),
            pltpu.VMEM((m, tokens, chans), BF16),
            pltpu.VMEM((m, tokens, chans), BF16),
            pltpu.VMEM((m, tokens, chans), BF16),
            pltpu.VMEM((m, tokens, chans), BF16),
            pltpu.VMEM((m, 8, tokens), F32),
            pltpu.VMEM((m, 8, tokens), F32),
            pltpu.VMEM((chans, tokens), BF16),
            pltpu.VMEM((chans, tokens), BF16),
            pltpu.VMEM((chans, tokens), BF16),
            pltpu.VMEM((n, pad, chans), F32),
            *sems(n, n, m, m, m, m),
            pltpu.SemaphoreType.DMA((4,)),
            *sems(n),
        ],
        compiler_params=pltpu.CompilerParams(
            collective_id=1, has_side_effects=True, vmem_limit_bytes=40 << 20
        ),
        name="back",
    )(result, d_rows, inputs, left, right, pack, aux, grad_out, cots, mixed, scale)
    return (
        layer_out,
        grad_in,
        tap_sum[:taps].T,
        tap_sum[taps],
        gate_sum[:2].T,
        grad_gate[None],
        grad_up[None],
        grad_down[None],
    )


def solution(mesh):
    return jax.shard_map(
        local,
        mesh=mesh,
        in_specs=(
            P("exp", "ctx"),
            P("exp", None),
            P("exp"),
            P("ctx", None),
            P("ctx", None),
            P("ctx", None, "exp"),
            P("ctx", None, "exp"),
            P("ctx", "exp", None),
            P("exp", "ctx"),
        ),
        out_specs=(
            P("exp", "ctx"),
            P("exp", "ctx"),
            P("exp", None),
            P("exp"),
            P("ctx", None),
            P("ctx", None, "exp"),
            P("ctx", None, "exp"),
            P("ctx", "exp", None),
        ),
        check_vma=False,
    )
```

profile of v0, /device:TPU:0, one launch (start us, length us, event | category | flops | bytes accessed | tf_op | source)
XLA Modules:
  0.0 84.7 jit_solution(4032520844724396359)
XLA Ops:
  0.6 0.0 copy-start
  0.6 0.8 broadcast_in_dim.20
  1.5 0.7 convert_element_type.28
  2.1 0.7 pad_maximum_fusion.1
  2.8 0.8 pad_maximum_fusion
  3.6 0.1 copy.25.aux_ref
  3.7 0.1 copy.24.pack_ref
  3.8 0.0 copy-start.1
  3.8 0.8 copy-done.1
  4.6 0.0 copy-start.2
  4.6 0.8 copy-done.2
  5.5 0.0 copy-start.3
  5.5 27.7 %front.1 = (bf16[256,1024]{1,0:T(8,128)(2,1)S(1)}, bf16[256,1024]{1,0:T(8,128)(2,1)S(1)}, bf16[256,128]{1,0:T(8,128)(2,1)S(1)}, f32[8,128]{1,0:T(8,128)S(1)}, bf...) custom-call(bf16[256,128]{1,0:T(8,128)(2,1)S(1)} %copy-done.1, ...), custom_call_target="tpu_custom_call" | custom-call | tf_op jit(solution)/shard_map/front/pallas_call | solution.py:315
  33.2 2.4 %fusion = f32[256,1024]{1,0:T(8,128)S(1)} fusion(bf16[256,1024]{1,0:T(8,128)(2,1)S(1)} %get-tuple-element.20, bf16[1,1024,1024]{2,1,0:T(8,128)(2,1)} %param.16), kind=kOutput, calls=%fused_computation | convolution fusion | flops 536870912 | bytes 3670016 | tf_op jit(solution)/shard_map/dot_general | solution.py:347
  35.6 0.0 copy-done.3
  35.6 0.7 fusion.6
  36.4 0.0 copy-done
  36.4 0.0 copy-start.4
  36.4 1.2 %multiply_convert_fusion.1 = (bf16[256,1024]{1,0:T(8,128)(2,1)S(1)}, bf16[256,1024]{1,0:T(8,128)(2,1)S(1)}, bf16[256,1024]{1,0:T(8,128)(2,1)S(1)}) fusion(f32[256,1024]{1,0:T(8,128)S(1)} %fusion, f32[256,1024]{1,0:T(8,128)S(1)} %fusion.6, bf16[256,1024]{1,0:T(8,128)(2,1)S(1)} %get-tuple-element.19, bf16[1,1024,1024]{2,1,0:T(8,128)(2,1)S(1)} %copy-done), kind=kOutput, calls=%fused_computation.19 | convolution fusion | flops 541065216 | bytes 6291456 | tf_op jit(solution)/shard_map/dot_general | solution.py:342
  37.6 0.4 copy-done.4
  38.0 0.7 fusion.15.y_ref
  38.7 2.1 %convert_bitcast_fusion = bf16[1,1024,1024]{2,1,0:T(8,128)(2,1)} fusion(bf16[256,1024]{1,0:T(8,128)(2,1)S(1)} %get-tuple-element.31, bf16[256,1024]{1,0:T(8,128)(2,1)S(1)} %get-tuple-element.20), kind=kOutput, calls=%fused_computation.12 | convolution fusion | flops 537919488 | bytes 3145728 | tf_op jit(solution)/shard_map/dot_general | solution.py:353
  40.8 0.7 fusion.4
  41.5 0.8 fusion.18.dx_ref
  42.3 35.3 %back.1 = (bf16[256,128]{1,0:T(8,128)(2,1)S(1)}, bf16[256,128]{1,0:T(8,128)(2,1)S(1)}, f32[32,256]{1,0:T(8,128)S(1)}, f32[8,128]{1,0:T(8,128)S(1)}) custom-call(bf16[256,1024]{1,0:T(8,128)(2,1)S(1)} %fusion.15.y_ref, bf16[256,1024]{1,0:T(8,128)(2,1)S(1)} %fusion.18.dx_ref, bf16[256,128]{1,0:T(8,128)(2,1)S(1)} %copy-done.1, ...), custom_call_target="tpu_custom_call" | custom-call | tf_op jit(solution)/shard_map/back/pallas_call | solution.py:356
  77.6 0.6 slice_bitcast_fusion.1
  78.2 0.6 slice.10
  78.7 0.6 slice_bitcast_fusion
  79.3 2.1 %convert_bitcast_fusion.2 = bf16[1,1024,1024]{2,1,0:T(8,128)(2,1)} fusion(bf16[256,1024]{1,0:T(8,128)(2,1)S(1)} %get-tuple-element.19, bf16[256,1024]{1,0:T(8,128)(2,1)S(1)} %get-tuple-element.30), kind=kOutput, calls=%fused_computation.14 | convolution fusion | flops 537919488 | bytes 3145728 | tf_op jit(solution)/shard_map/dot_general | solution.py:354
  81.4 2.1 %convert_bitcast_fusion.1 = bf16[1,1024,1024]{2,1,0:T(8,128)(2,1)} fusion(bf16[256,1024]{1,0:T(8,128)(2,1)S(1)} %get-tuple-element.19, bf16[256,1024]{1,0:T(8,128)(2,1)S(1)} %get-tuple-element.32), kind=kOutput, calls=%fused_computation.13 | convolution fusion | flops 537919488 | bytes 3145728 | tf_op jit(solution)/shard_map/dot_general | solution.py:355
  83.5 0.6 copy.30
  84.1 0.6 copy.31
Async XLA Ops:
  0.6 35.7 %copy-start = (bf16[1,1024,1024]{2,1,0:T(8,128)(2,1)S(1)}, bf16[1,1024,1024]{2,1,0:T(8,128)(2,1)}, u32[]{:S(2)}) copy-start(bf16[1,1024,1024]{2,1,0:T(8,128)(2,1)} %param.14) | copy-start | bytes 6291460
  3.8 0.8 copy-start.1
  4.6 0.8 copy-start.2
  5.5 30.1 %copy-start.3 = (bf16[1,1024,1024]{2,1,0:T(8,128)(2,1)S(1)}, bf16[1,1024,1024]{2,1,0:T(8,128)(2,1)}, u32[]{:S(2)}) copy-start(bf16[1,1024,1024]{2,1,0:T(8,128)(2,1)} %param.15) | copy-start | bytes 6291460
  36.4 1.6 %copy-start.4 = (bf16[1,1024,1024]{2,1,0:T(8,128)(2,1)S(1)}, bf16[1,1024,1024]{2,1,0:T(8,128)(2,1)}, u32[]{:S(2)}) copy-start(bf16[1,1024,1024]{2,1,0:T(8,128)(2,1)} %param.16) | copy-start | bytes 6291460
where the time goes:
time: 85.2 us; the launch traced here: 84.7 us
  Pallas kernels  63 us (74%)
  matrix products  12.8 us (15%)
  local copies, waits for them, and re-layouts  5.29 us (6%)
  other arithmetic  2.94 us (3%)
    pallas_call x1, Pallas kernels, local(): pl.pallas_call(functools.partial(back, n, m, taps, capacity), out_shape=(...  35.3 us
    pallas_call x1, Pallas kernels, local(): pl.pallas_call(functools.partial(front, n, m, taps, capacity), out_shape=...  27.7 us
    unnamed x12, local copies, waits for them, and re-layouts  3.34 us
    dot_general x1, matrix products, local(): lax.dot_general(rdy, weight_down, LAST, preferred_element_type=F32)  2.38 us
    dot_general x1, matrix products, local(): lax.dot_general(rx, d_gate, FIRST, preferred_element_type=F32).astype(BF16)  2.07 us
    dot_general x1, matrix products, local(): lax.dot_general(hidden, rdy, FIRST, preferred_element_type=F32).astype(BF16)  2.07 us
    dot_general x1, matrix products, local(): lax.dot_general(rx, d_up, FIRST, preferred_element_type=F32).astype(BF16)  2.07 us

commit v1 on v0

v1 whole, which is shorter than its diff:
```python
import functools
import jax
import jax.numpy as jnp
from jax import lax
from jax.experimental import pallas as pl
from jax.experimental.pallas import tpu as pltpu
from jax.sharding import PartitionSpec as P

EPS = 1e-05
EDGE = 16
MESH = pl.DeviceIdType.MESH
F32, BF16 = jnp.float32, jnp.bfloat16
LAST = (((1,), (1,)), ((), ()))
FIRST = (((0,), (0,)), ((), ()))


def dot(a, b, dims=(((1,), (0,)), ((), ()))):
    return lax.dot_general(a, b, dims, preferred_element_type=F32)


def announce(n, m):
    c, e = lax.axis_index("ctx"), lax.axis_index("exp")
    barrier = pltpu.get_barrier_semaphore()

    def ctx_peer(k, _):
        pl.semaphore_signal(barrier, inc=1, device_id=(lax.rem(c + k, n), e), device_id_type=MESH)
        return 0

    def exp_peer(k, _):
        pl.semaphore_signal(barrier, inc=1, device_id=(c, lax.rem(e + k, m)), device_id_type=MESH)
        return 0

    lax.fori_loop(1, n, ctx_peer, 0)
    lax.fori_loop(1, m, exp_peer, 0)
    return barrier


class Exchange:
    def __init__(self, axis, size, src, dst, send, recv):
        self.axis, self.size, self.src, self.dst = axis, size, src, dst
        self.send, self.recv = send, recv
        self.me = lax.axis_index(axis)

    def copy(self, k, slot):
        peer = lax.rem(self.me + k, self.size)
        if self.axis == "ctx":
            where = (peer, lax.axis_index("exp"))
        else:
            where = (lax.axis_index("ctx"), peer)
        slot = peer if slot is None else slot
        return pltpu.make_async_remote_copy(
            src_ref=self.src(peer),
            dst_ref=self.dst(slot),
            send_sem=self.send.at[peer],
            recv_sem=self.recv.at[slot],
            device_id=where,
            device_id_type=MESH,
        )

    def each(self, act):
        def body(k, _):
            act(k)
            return 0

        lax.fori_loop(1, self.size, body, 0)

    def start(self):
        self.each(lambda k: self.copy(k, self.me).start())

    def arrive(self):
        self.each(lambda k: self.copy(k, None).wait_recv())

    def sent(self):
        self.each(lambda k: self.copy(k, self.me).wait_send())


class Halo:
    def __init__(self, n, edges, left, right, sems):
        c, e = lax.axis_index("ctx"), lax.axis_index("exp")
        up, down = lax.rem(c + 1, n), lax.rem(c + n - 1, n)
        make = pltpu.make_async_remote_copy
        self.copies = [
            make(edges.at[1], left, sems.at[0], sems.at[1], device_id=(up, e), device_id_type=MESH),
            make(edges.at[0], right, sems.at[2], sems.at[3], device_id=(down, e), device_id_type=MESH),
        ]

    def start(self):
        for copy in self.copies:
            copy.start()

    def arrive(self):
        for copy in self.copies:
            copy.wait_recv()

    def sent(self):
        for copy in self.copies:
            copy.wait_send()


def column(row):
    return jnp.transpose(jnp.broadcast_to(row, (128, row.shape[1])))


def turn_row(col):
    return jnp.transpose(jnp.broadcast_to(col, (col.shape[0], 128)))[:1]


def windows(block, base, taps):
    rows = block.shape[0]
    for b in range(8):
        offs = [o for o in range(base, base + taps) if o % 8 == b]
        if offs:
            yield b, (block if b == 0 else pltpu.roll(block, rows - b, axis=0)), offs


def layer(n, m, taps, cap, nc,
          x_any, tap_any, gain_any, route_any, prob_any, cot_any, wg_any, wu_any, wd_any,
          lo_ref, gin_ref, tapo_ref, gaino_ref, gateo_ref, gwg_ref, gwu_ref, gwd_ref,
          x_s, tap_s, gain_s, route_s, prob_s, cot_s, wg, wu, wd,
          xp, xs, xe, hl, hr, cots, mx, side, pt, pb, p0s, p1s, gs, gc, sc,
          sdy, sx, rdy, rx, dh, ga, ua, hid, dg, du, sdx, sy, bdx, by,
          zdx, zy, rdx, ry, dots, norm, dmp, de, dl, dr, tp,
          lsem, hs, hs2, *sem):
    me, mine = lax.axis_index("ctx"), lax.axis_index("exp")
    chans, tokens = x_s.shape
    slots = pt.shape[0]
    width, inner = wg.shape
    cw = chans // nc
    it = iter(sem)
    own = pl.ds(pl.multiple_of(me * cap, cap), cap)

    def pair():
        return next(it), next(it)

    def spans(h, k):
        return slice(k * cw, (k + 1) * cw)

    def chan_rows(ref, h, cols=slice(None)):
        if nc == 1:
            return ref[:, cols]
        return jnp.concatenate(
            [ref[k * chans + h * cw : k * chans + (h + 1) * cw, cols] for k in range(m)], axis=0
        )

    def natural(ref, lo, hi):
        if nc == 1:
            return ref[0, :, lo:hi]
        return jnp.concatenate(
            [ref[h, :, spans(h, k)] for k in range(lo // chans, hi // chans) for h in range(nc)], axis=1
        )

    def rows(ref, h):
        return lambda p: ref.at[h, pl.ds(pl.multiple_of(p * cap, cap), cap)]

    def spread(matrix, pieces):
        if cw % 128 == 0:
            full = dot(matrix, jnp.concatenate(pieces, axis=1))
            return [full[:, k * cw : (k + 1) * cw] for k in range(len(pieces))]
        return [dot(matrix, piece) for piece in pieces]

    barrier = announce(n, m)
    loads = [
        pltpu.make_async_copy(src, dst, lsem.at[i])
        for i, (src, dst) in enumerate(
            [(x_any, x_s), (cot_any, cot_s), (route_any, route_s), (prob_any, prob_s),
             (tap_any, tap_s), (gain_any, gain_s)]
        )
    ]
    weights = [
        pltpu.make_async_copy(src.at[0], dst, lsem.at[6 + i])
        for i, (src, dst) in enumerate([(wd_any, wd), (wg_any, wg), (wu_any, wu)])
    ]
    for load in loads:
        load.start()
    for load in weights:
        load.start()
    loads[0].wait()
    loads[1].wait()
    x_t = jnp.transpose(x_s[...].astype(F32))
    xp[EDGE : EDGE + tokens, :] = x_t
    xe[0] = x_t[:EDGE].astype(BF16)
    xe[1] = x_t[tokens - EDGE :].astype(BF16)
    cot_t = jnp.transpose(cot_s[...].astype(F32)).astype(BF16)
    for h in range(nc):
        cots[h, mine] = cot_t[:, h * cw : (h + 1) * cw]
    pl.semaphore_wait(barrier, n + m - 2)

    halo = Halo(n, xe, hl, hr, hs)
    halo.start()
    gather_cot = []
    for h in range(nc):
        gather_cot.append(
            Exchange("exp", m, lambda p, h=h: cots.at[h, mine], lambda s, h=h: cots.at[h, s], *pair())
        )
        gather_cot[h].start()

    for load in loads[2:]:
        load.wait()
    ids = lax.broadcasted_iota(jnp.int32, (n, tokens), 0)
    named = [route_s[k : k + 1, :] for k in range(2)]
    probs = [prob_s[k : k + 1, :] for k in range(2)]
    hot = [(ids == r).astype(F32) for r in named]
    earlier = lax.broadcasted_iota(jnp.int32, (tokens, tokens), 0) < lax.broadcasted_iota(
        jnp.int32, (tokens, tokens), 1
    )
    count = dot((hot[0] + hot[1]).astype(BF16), earlier.astype(F32).astype(BF16))
    place = lax.broadcasted_iota(jnp.int32, (slots, tokens), 0)
    picks = []
    for r, one in zip(named, hot):
        slot = jnp.sum(count * one, axis=0, keepdims=True).astype(jnp.int32)
        picks.append((place == r * cap + slot).astype(F32))
    pt[...] = (picks[0] + picks[1]).astype(BF16)
    gate_slot = jnp.sum(picks[0] * probs[0] + picks[1] * probs[1], axis=1, keepdims=True)
    gs[...] = jnp.broadcast_to(gate_slot, gs.shape)
    turned = [jnp.transpose(p) for p in picks]
    p0s[...] = turned[0].astype(BF16)
    p1s[...] = turned[1].astype(BF16)
    pb[...] = (turned[0] + turned[1]).astype(BF16)
    gc[0] = column(probs[0])
    gc[1] = column(probs[1])
    gain_row = gain_s[...].astype(F32)
    side[mine] = jnp.zeros(side.shape[1:], F32)
    dots[mine] = jnp.zeros(dots.shape[1:], F32)

    halo.arrive()
    xp[:EDGE, :] = hl[...].astype(F32)
    xp[EDGE + tokens :, :] = hr[...].astype(F32)
    base = EDGE - taps // 2
    span = tokens + 24
    squares = jnp.zeros((tokens, 1), F32)
    for h in range(nc):
        lanes = slice(h * cw, (h + 1) * cw)
        block = xp[:, lanes]
        acc = xp[EDGE : EDGE + tokens, lanes]
        for b, moved, offs in windows(block, base, taps):
            xs[b, :, lanes] = moved[:span]
            for o in offs:
                acc = acc + tap_s[o - base : o - base + 1, lanes] * moved[o - b : o - b + tokens]
        mixed = acc.astype(BF16)
        mx[h, mine] = mixed
        mixed = mixed.astype(F32)
        squares = squares + jnp.sum(mixed * mixed, axis=1, keepdims=True)
        side[mine, 1 + h : 2 + h, :cw] = gain_row[:, lanes]
    side[mine, 0:1, :tokens] = turn_row(squares)
    share = Exchange("exp", m, lambda p: side.at[mine], lambda s: side.at[s], *pair())
    share.start()
    gather_x = []
    for h in range(nc):
        gather_x.append(
            Exchange("exp", m, lambda p, h=h: mx.at[h, mine], lambda s, h=h: mx.at[h, s], *pair())
        )
        gather_x[h].start()

    send_dy, send_x = [], []
    for h in range(nc):
        gather_cot[h].arrive()
        for k, part in enumerate(spread(pt[...], [cots[h, k] for k in range(m)])):
            sdy[h, :, spans(h, k)] = (part * gs[:, :cw]).astype(BF16)
        send_dy.append(Exchange("ctx", n, rows(sdy, h), rows(rdy, h), *pair()))
        send_dy[h].start()
        rdy[h, own, :] = sdy[h, own, :]
    share.arrive()
    total = jnp.sum(side[...], axis=0)[:1, :tokens]
    sc[...] = column(lax.rsqrt(total / width + EPS))
    for h in range(nc):
        gather_x[h].arrive()
        normed = [
            (mx[h, k].astype(F32) * side[k, 1 + h : 2 + h, :cw] * sc[:, :cw]).astype(BF16) for k in range(m)
        ]
        for k, part in enumerate(spread(pt[...], normed)):
            sx[h, :, spans(h, k)] = part.astype(BF16)
        send_x.append(Exchange("ctx", n, rows(sx, h), rows(rx, h), *pair()))
        send_x[h].start()
        rx[h, own, :] = sx[h, own, :]

    tile = min(256, inner)
    tiles = [slice(f, f + tile) for f in range(0, inner, tile)]
    weights[0].wait()
    for h in range(nc):
        send_dy[h].arrive()
    d_y = natural(rdy, 0, width)
    for f in tiles:
        dh[:, f] = dot(d_y, wd[f, :], LAST)
    weights[1].wait()
    weights[2].wait()
    for h in range(nc):
        send_x[h].arrive()
        for f in tiles:
            g = dot(rx[h], chan_rows(wg, h, f))
            u = dot(rx[h], chan_rows(wu, h, f))
            ga[:, f] = g if h == 0 else ga[:, f] + g
            ua[:, f] = u if h == 0 else ua[:, f] + u
            if h == nc - 1:
                step = 32
                for r in range(0, slots, step):
                    at = slice(r, r + step)
                    g, u, d = ga[at, f], ua[at, f], dh[at, f]
                    sigma = jax.nn.sigmoid(g)
                    swish = g * sigma
                    hid[at, f] = (swish * u).astype(BF16)
                    dg[at, f] = (d * u * sigma * (1.0 + g * (1.0 - sigma))).astype(BF16)
                    du[at, f] = (d * swish).astype(BF16)

    group = max(1, min(m, 256 // cw))
    send_dx, send_y = [], []
    for h in range(nc):
        for k in range(0, m, group):
            if nc == 1:
                at = slice(k * cw, (k + group) * cw)
                w1, w2 = wg[at, :], wu[at, :]
            else:
                w1, w2 = [
                    jnp.concatenate(
                        [w[j * chans + h * cw : j * chans + (h + 1) * cw, :] for j in range(k, k + group)], axis=0
                    )
                    for w in (wg, wu)
                ]
            part = dot(dg[...], w1, LAST) + dot(du[...], w2, LAST)
            sdx[h, :, k * cw : (k + group) * cw] = part.astype(BF16)
        send_dx.append(Exchange("ctx", n, rows(sdx, h), rows(bdx, h), *pair()))
        send_dx[h].start()
        bdx[h, own, :] = sdx[h, own, :]
    for h in range(nc):
        for k in range(0, m, group):
            if nc == 1:
                w = wd[:, k * cw : (k + group) * cw]
            else:
                w = jnp.concatenate(
                    [wd[:, j * chans + h * cw : j * chans + (h + 1) * cw] for j in range(k, k + group)], axis=1
                )
            sy[h, :, k * cw : (k + group) * cw] = dot(hid[...], w).astype(BF16)
        send_y.append(Exchange("ctx", n, rows(sy, h), rows(by, h), *pair()))
        send_y[h].start()
        by[h, own, :] = sy[h, own, :]

    for f in tiles:
        gwd_ref[f, :] = dot(hid[:, f], natural(rdy, 0, width), FIRST).astype(BF16)
    for lo in range(0, width, 256):
        part = natural(rx, lo, lo + 256)
        gwg_ref[lo : lo + 256, :] = dot(part, dg[...], FIRST).astype(BF16)
        gwu_ref[lo : lo + 256, :] = dot(part, du[...], FIRST).astype(BF16)

    sum_dx, sum_y = [], []
    weighted = jnp.zeros((tokens, cw), F32)
    sum_norm = Exchange("exp", m, lambda p: norm.at[mine], lambda s: norm.at[s], *pair())
    for h in range(nc):
        send_dx[h].arrive()
        full = dot(pb[...], bdx[h])
        for k in range(m):
            part = full[:, spans(h, k)]
            zdx[h, k] = part.astype(BF16)
            weighted = weighted + part * mx[h, k].astype(F32) * side[k, 1 + h : 2 + h, :cw]
        if h == nc - 1:
            row = turn_row(jnp.sum(weighted, axis=1, keepdims=True))
            norm[mine] = jnp.broadcast_to(row, norm.shape[1:])
            sum_norm.start()
        sum_dx.append(
            Exchange("exp", m, lambda p, h=h: zdx.at[h, p], lambda s, h=h: rdx.at[h, s], *pair())
        )
        sum_dx[h].start()
        rdx[h, mine] = zdx[h, mine]

    d0 = jnp.zeros((tokens, cw), F32)
    d1 = jnp.zeros((tokens, cw), F32)

    def combine(h, d0, d1):
        send_y[h].arrive()
        y0, y1 = dot(p0s[...], by[h]), dot(p1s[...], by[h])
        for k in range(m):
            a, b = y0[:, spans(h, k)], y1[:, spans(h, k)]
            zy[h, k] = (a * gc[0, :, :cw] + b * gc[1, :, :cw]).astype(BF16)
            cot = cots[h, k].astype(F32)
            d0, d1 = d0 + a * cot, d1 + b * cot
        sum_y.append(
            Exchange("exp", m, lambda p, h=h: zy.at[h, p], lambda s, h=h: ry.at[h, s], *pair())
        )
        sum_y[h].start()
        ry[h, mine] = zy[h, mine]
        return d0, d1

    for h in range(nc - 1):
        d0, d1 = combine(h, d0, d1)

    for h in range(nc):
        sum_dx[h].arrive()
    sum_norm.arrive()
    q = column(jnp.sum(norm[...], axis=0)[:1])
    scale = sc[...]
    pull = q * scale * scale * scale / width
    for h in range(nc):
        lanes = slice(h * cw, (h + 1) * cw)
        dn = jnp.sum(rdx[h].astype(F32), axis=0)
        mixed = mx[h, mine].astype(F32)
        dm = cots[h, mine].astype(F32) + gain_row[:, lanes] * dn * scale[:, :cw] - mixed * pull[:, :cw]
        dmp[EDGE : EDGE + tokens, lanes] = dm
        de[0, :, lanes] = dm[:EDGE].astype(BF16)
        de[1, :, lanes] = dm[tokens - EDGE :].astype(BF16)
        tp[me, taps : taps + 1, lanes] = jnp.sum(
            dn * mixed * scale[:, :cw], axis=0, keepdims=True
        ).astype(BF16)
    halo_d = Halo(n, de, dl, dr, hs2)
    halo_d.start()
    d0, d1 = combine(nc - 1, d0, d1)
    dots[mine, 0:1, :] = turn_row(jnp.sum(d0, axis=1, keepdims=True))
    dots[mine, 1:2, :] = turn_row(jnp.sum(d1, axis=1, keepdims=True))
    sum_dots = Exchange("exp", m, lambda p: dots.at[mine], lambda s: dots.at[s], *pair())
    sum_dots.start()

    for h in range(nc):
        lanes = slice(h * cw, (h + 1) * cw)
        dm = dmp[EDGE : EDGE + tokens, lanes]
        for j in range(taps):
            o = base + j
            b = o % 8
            term = jnp.sum(dm * xs[b, o - b : o - b + tokens, lanes], axis=0, keepdims=True)
            tp[me, j : j + 1, lanes] = term.astype(BF16)
    sum_taps = Exchange("ctx", n, lambda p: tp.at[me], lambda s: tp.at[s], *pair())
    sum_taps.start()
    halo_d.arrive()
    dmp[:EDGE, :] = dl[...].astype(F32)
    dmp[EDGE + tokens :, :] = dr[...].astype(F32)
    low = EDGE + taps // 2 - (taps - 1)
    for h in range(nc):
        lanes = slice(h * cw, (h + 1) * cw)
        block = dmp[:, lanes]
        acc = dmp[EDGE : EDGE + tokens, lanes]
        for b, moved, offs in windows(block, low, taps):
            for o in offs:
                j = EDGE + taps // 2 - o
                acc = acc + tap_s[j : j + 1, lanes] * moved[o - b : o - b + tokens]
        gin_ref[lanes, :] = jnp.transpose(acc).astype(BF16)
    for h in range(nc):
        sum_y[h].arrive()
        out = mx[h, mine].astype(F32) + jnp.sum(ry[h].astype(F32), axis=0)
        lo_ref[h * cw : (h + 1) * cw, :] = jnp.transpose(out).astype(BF16)
    sum_dots.arrive()
    gateo_ref[...] = jnp.sum(dots[...], axis=0)[:2]
    sum_taps.arrive()
    grads = jnp.sum(tp[...].astype(F32), axis=0)
    tapo_ref[...] = grads[:taps]
    gaino_ref[...] = grads[taps : taps + 1]
    for done in (halo, halo_d, share, sum_norm, sum_dots, sum_taps):
        done.sent()
    for group in (gather_cot, gather_x, send_dy, send_x, send_dx, send_y, sum_dx, sum_y):
        for done in group:
            done.sent()


def finish(*refs):
    count = (len(refs) - 1) // 2
    sem = refs[-1]
    copies = [
        pltpu.make_async_copy(refs[i], refs[count + i], sem.at[i]) for i in range(count)
    ]
    for copy in copies:
        copy.start()
    for copy in copies:
        copy.wait()


def local(inputs, conv_taps, norm_gain, routes, gate_probs, w_gate, w_up, w_down, grad_out):
    chans, tokens = inputs.shape
    taps = conv_taps.shape[1]
    width, inner = w_gate.shape[1:]
    n, m = lax.axis_size("ctx"), lax.axis_size("exp")
    cap = max(tokens // 8, (2 * tokens + n - 1) // n)
    slots = n * cap
    pad = -(-(taps + 1) // 16) * 16
    nc = max(1, chans // 128)
    cw = chans // nc
    vmem = pl.BlockSpec(memory_space=pltpu.VMEM)
    hbm = pl.BlockSpec(memory_space=pl.ANY)
    shape = jax.ShapeDtypeStruct
    dma = pltpu.SemaphoreType.DMA
    V = pltpu.VMEM
    outs = (
        shape((chans, tokens), BF16),
        shape((chans, tokens), BF16),
        shape((taps, chans), F32),
        shape((1, chans), F32),
        shape((2, tokens), F32),
        shape((width, inner), BF16),
        shape((width, inner), BF16),
        shape((inner, width), BF16),
    )
    sizes = [m] * nc + [m] + [m] * nc + [n] * (2 * nc) + [n] * (2 * nc) + [m]
    sizes += [m] * nc + [m] * nc + [m] + [n]
    big = V((nc, slots, m * cw), BF16)
    results = pl.pallas_call(
        functools.partial(layer, n, m, taps, cap, nc),
        out_shape=outs,
        in_specs=[hbm] * 9,
        out_specs=(vmem,) * 8,
        scratch_shapes=[
            V((chans, tokens), BF16), V((taps, chans), F32), V((1, chans), BF16),
            V((2, tokens), jnp.int32), V((2, tokens), F32), V((chans, tokens), BF16),
            V((width, inner), BF16), V((width, inner), BF16), V((inner, width), BF16),
            V((tokens + 2 * EDGE, chans), F32), V((8, tokens + 24, chans), F32),
            V((2, EDGE, chans), BF16), V((EDGE, chans), BF16), V((EDGE, chans), BF16),
            V((nc, m, tokens, cw), BF16), V((nc, m, tokens, cw), BF16),
            V((m, 8, max(tokens, cw)), F32),
            V((slots, tokens), BF16), V((tokens, slots), BF16), V((tokens, slots), BF16),
            V((tokens, slots), BF16),
            V((slots, 128), F32), V((2, tokens, 128), F32), V((tokens, 128), F32),
            big, big, big, big,
            V((slots, inner), F32), V((slots, inner), F32), V((slots, inner), F32),
            V((slots, inner), BF16), V((slots, inner), BF16), V((slots, inner), BF16),
            big, big, big, big,
            V((nc, m, tokens, cw), BF16), V((nc, m, tokens, cw), BF16),
            V((nc, m, tokens, cw), BF16), V((nc, m, tokens, cw), BF16),
            V((m, 8, tokens), F32), V((m, 8, tokens), F32),
            V((tokens + 2 * EDGE, chans), F32),
            V((2, EDGE, chans), BF16), V((EDGE, chans), BF16), V((EDGE, chans), BF16),
            V((n, pad, chans), BF16),
            dma((9,)), dma((4,)), dma((4,)),
            *[dma((s,)) for s in sizes for _ in range(2)],
        ],
        compiler_params=pltpu.CompilerParams(
            collective_id=0, has_side_effects=True, vmem_limit_bytes=48 << 20
        ),
        name="layer",
    )(inputs, conv_taps.T, norm_gain[None], routes.T, gate_probs.T, grad_out, w_gate, w_up, w_down)
    results = pl.pallas_call(
        finish,
        out_shape=outs,
        in_specs=[vmem] * 8,
        out_specs=(hbm,) * 8,
        scratch_shapes=[dma((8,))],
        compiler_params=pltpu.CompilerParams(vmem_limit_bytes=16 << 20),
        name="finish",
    )(*results)
    layer_out, grad_in, grad_taps, grad_gain, grad_gates, grad_gate, grad_up, grad_down = results
    return (
        layer_out,
        grad_in,
        grad_taps.T,
        grad_gain[0],
        grad_gates.T,
        grad_gate[None],
        grad_up[None],
        grad_down[None],
    )


def solution(mesh):
    return jax.shard_map(
        local,
        mesh=mesh,
        in_specs=(
            P("exp", "ctx"),
            P("exp", None),
            P("exp"),
            P("ctx", None),
            P("ctx", None),
            P("ctx", None, "exp"),
            P("ctx", None, "exp"),
            P("ctx", "exp", None),
            P("exp", "ctx"),
        ),
        out_specs=(
            P("exp", "ctx"),
            P("exp", "ctx"),
            P("exp", None),
            P("exp"),
            P("ctx", None),
            P("ctx", None, "exp"),
            P("ctx", None, "exp"),
            P("ctx", "exp", None),
        ),
        check_vma=False,
    )
```

time: 85.2 us -> 62 us (0.73)
  matrix products: 12.8 us -> 0 us
  Pallas kernels: 63 us -> 55 us
  other arithmetic: 2.94 us -> 0 us
    dot_general x9 -> x0, matrix products: 12.8 us -> none  [the longest x1 2.38 us: local(): lax.dot_general(rdy, weight_down, LAST, preferred_element_type=F32)]
    pallas_call x2, Pallas kernels: 63 us -> 55 us  [the longest x1 52.2 us: local(): pl.pallas_call(functools.partial(layer, n, m, taps, cap, nc), out_shape=o...]
    unnamed x12, local copies, waits for them, and re-layouts: 3.34 us -> 5.38 us
    concatenate x2 -> x0, other arithmetic: 1.45 us -> none  [the longest x1 0.77 us: local(): pack = jnp.concatenate([conv_taps, norm_gain.astype(F32)[:, None]], axis=1)]
    transpose x2 -> x0, local copies, waits for them, and re-layouts: 1.18 us -> none  [the longest x1 0.62 us: local(): tap_sum[:taps]]
where the time goes in v1:
time: 62 us; the launch traced here: 61.7 us
  Pallas kernels  55 us (89%)
  local copies, waits for them, and re-layouts  6.04 us (10%)
  between operations  0.65 us (1%)
    pallas_call x1, Pallas kernels, local(): pl.pallas_call(functools.partial(layer, n, m, taps, cap, nc), out_shape=o...  52.2 us
    unnamed x12, local copies, waits for them, and re-layouts  5.38 us
    pallas_call x1, Pallas kernels, local(): pl.pallas_call(finish, out_shape=outs, in_specs=[vmem] * 8, out_specs=(hb...  2.83 us

profile of v1, /device:TPU:0, one launch (start us, length us, event | category | flops | bytes accessed | tf_op | source)
XLA Modules:
  0.0 61.7 jit_solution(3442568875350606228)
XLA Ops:
  0.6 0.7 %broadcast_in_dim.12.gain_any = bf16[1,256]{1,0:T(2,128)(2,1)S(1)} reshape(bf16[256]{0:T(256)(128)(2,1)} %param.11) | data formatting | bytes 1024 | tf_op jit(solution)/shard_map/broadcast_in_dim | solution.py:522
  1.3 0.0 copy-start.1
  1.3 0.8 %copy-done.1 = bf16[256,128]{1,0:T(8,128)(2,1)S(1)} copy-done((bf16[256,128]{1,0:T(8,128)(2,1)S(1)}, bf16[256,128]{1,0:T(8,128)(2,1)}, u32[]{:S(2)}) %copy-start.1) | copy-done | bytes 65560
  2.1 0.0 copy-start.2
  2.1 0.8 %copy-done.2 = bf16[256,128]{1,0:T(8,128)(2,1)S(1)} copy-done((bf16[256,128]{1,0:T(8,128)(2,1)S(1)}, bf16[256,128]{1,0:T(8,128)(2,1)}, u32[]{:S(2)}) %copy-start.2) | copy-done | bytes 65560
  3.0 0.0 copy-start.3
  3.0 0.8 %copy-done.3 = f32[256,31]{0,1:T(8,128)S(1)} copy-done((f32[256,31]{0,1:T(8,128)S(1)}, f32[256,31]{0,1:T(8,128)}, u32[]{:S(2)}) %copy-start.3) | copy-done | bytes 31768
  3.7 0.0 copy-start.4
  3.7 0.7 %copy-done.4 = s32[128,2]{0,1:T(2,128)S(1)} copy-done((s32[128,2]{0,1:T(2,128)S(1)}, s32[128,2]{0,1:T(2,128)}, u32[]{:S(2)}) %copy-start.4) | copy-done | bytes 1048
  4.4 0.0 copy-start.5
  4.4 0.7 %copy-done.5 = f32[128,2]{0,1:T(2,128)S(1)} copy-done((f32[128,2]{0,1:T(2,128)S(1)}, f32[128,2]{0,1:T(2,128)}, u32[]{:S(2)}) %copy-start.5) | copy-done | bytes 1048
  5.1 52.2 %layer.1 = (bf16[256,128]{1,0:T(8,128)(2,1)S(1)}, bf16[256,128]{1,0:T(8,128)(2,1)S(1)}, f32[31,256]{1,0:T(8,128)S(1)}, f32[1,256]{1,0:T(1,128)S(1)}, f32[2,128]{...) custom-call(bf16[256,128]{1,0:T(8,128)(2,1)S(1)} %copy-done.1, ...), custom_call_target="tpu_custom_call" | custom-call | tf_op jit(solution)/shard_map/layer/pallas_call | solution.py:489
  57.3 0.0 copy-start
  57.3 1.6 %copy-done = bf16[1024,1024]{1,0:T(8,128)(2,1)S(1)} copy-done((bf16[1024,1024]{1,0:T(8,128)(2,1)S(1)}, bf16[1024,1024]{1,0:T(8,128)(2,1)}, u32[]{:S(2)}) %copy-start) | copy-done | bytes 2097176
  58.8 2.8 %finish.1 = (bf16[256,128]{1,0:T(8,128)(2,1)}, bf16[256,128]{1,0:T(8,128)(2,1)}, f32[31,256]{1,0:T(8,128)}, f32[1,256]{1,0:T(1,128)}, f32[2,128]{1,0:T(2,128)}, ...) custom-call(bf16[256,128]{1,0:T(8,128)(2,1)S(1)} %get-tuple-element.24.refs_0_, ...), custom_call_target="tpu_custom_call" | custom-call | tf_op jit(solution)/shard_map/finish/pallas_call | solution.py:523
Async XLA Ops:
  1.3 0.8 %copy-start.1 = (bf16[256,128]{1,0:T(8,128)(2,1)S(1)}, bf16[256,128]{1,0:T(8,128)(2,1)}, u32[]{:S(2)}) copy-start(bf16[256,128]{1,0:T(8,128)(2,1)} %x_any.1) | copy-start | bytes 196612
  2.1 0.8 %copy-start.2 = (bf16[256,128]{1,0:T(8,128)(2,1)S(1)}, bf16[256,128]{1,0:T(8,128)(2,1)}, u32[]{:S(2)}) copy-start(bf16[256,128]{1,0:T(8,128)(2,1)} %cot_any.1) | copy-start | bytes 196612
  3.0 0.8 %copy-start.3 = (f32[256,31]{0,1:T(8,128)S(1)}, f32[256,31]{0,1:T(8,128)}, u32[]{:S(2)}) copy-start(f32[256,31]{0,1:T(8,128)} %param.10) | copy-start | bytes 95236
  3.7 0.7 %copy-start.4 = (s32[128,2]{0,1:T(2,128)S(1)}, s32[128,2]{0,1:T(2,128)}, u32[]{:S(2)}) copy-start(s32[128,2]{0,1:T(2,128)} %param.12) | copy-start | bytes 3076
  4.4 0.7 %copy-start.5 = (f32[128,2]{0,1:T(2,128)S(1)}, f32[128,2]{0,1:T(2,128)}, u32[]{:S(2)}) copy-start(f32[128,2]{0,1:T(2,128)} %param.13) | copy-start | bytes 3076
  57.3 1.6 %copy-start = (bf16[1024,1024]{1,0:T(8,128)(2,1)S(1)}, bf16[1024,1024]{1,0:T(8,128)(2,1)}, u32[]{:S(2)}) copy-start(bf16[1024,1024]{1,0:T(8,128)(2,1)} %get-tuple-element.31.refs_7_) | copy-start | bytes 6291460

commit v2 on v1

--- a/solution.py
+++ b/solution.py
@@ -118,7 +118,7 @@
           lo_ref, gin_ref, tapo_ref, gaino_ref, gateo_ref, gwg_ref, gwu_ref, gwd_ref,
           x_s, tap_s, gain_s, route_s, prob_s, cot_s, wg, wu, wd,
           xp, xs, xe, hl, hr, cots, mx, side, pt, pb, p0s, p1s, gs, gc, sc,
-          sdy, sx, rdy, rx, dh, ga, ua, hid, dg, du, sdx, sy, bdx, by,
+          sdy, sx, rdy, rx, sxl, xa, xg, dh, ga, ua, hid, dg, du, sdx, sy, bdx, by, sl, rl, ol, bl,
           zdx, zy, rdx, ry, dots, norm, dmp, de, dl, dr, tp,
           lsem, hs, hs2, *sem):
     me, mine = lax.axis_index("ctx"), lax.axis_index("exp")
@@ -128,6 +128,9 @@
     cw = chans // nc
     it = iter(sem)
     own = pl.ds(pl.multiple_of(me * cap, cap), cap)
+    late = nc - 1 if nc > 1 else None
+    direct = [h for h in range(nc) if h != late]
+    span_all = m * cw
 
     def pair():
         return next(it), next(it)
@@ -149,8 +152,11 @@
             [ref[h, :, spans(h, k)] for k in range(lo // chans, hi // chans) for h in range(nc)], axis=1
         )
 
-    def rows(ref, h):
-        return lambda p: ref.at[h, pl.ds(pl.multiple_of(p * cap, cap), cap)]
+    def rows(ref, *h):
+        return lambda p: ref.at[(*h, pl.ds(pl.multiple_of(p * cap, cap), cap))]
+
+    def gain_of(k, h):
+        return side[k, 1 + h : 2 + h, :cw]
 
     def spread(matrix, pieces):
         if cw % 128 == 0:
@@ -218,7 +224,7 @@
     pb[...] = (turned[0] + turned[1]).astype(BF16)
     gc[0] = column(probs[0])
     gc[1] = column(probs[1])
-    gain_row = gain_s[...].astype(F32)
+    gain_row = gain_s[...].astype(F32).reshape(1, chans)
     side[mine] = jnp.zeros(side.shape[1:], F32)
     dots[mine] = jnp.zeros(dots.shape[1:], F32)
 
@@ -244,16 +250,26 @@
     side[mine, 0:1, :tokens] = turn_row(squares)
     share = Exchange("exp", m, lambda p: side.at[mine], lambda s: side.at[s], *pair())
     share.start()
-    gather_x = []
-    for h in range(nc):
-        gather_x.append(
+    if late is not None:
+        sxl[...] = dot(pt[...], mx[late, mine]).astype(BF16)
+        send_late_x = Exchange("ctx", n, rows(sxl), rows(xg, mine), *pair())
+        send_late_x.start()
+        xg[mine, own, :] = sxl[own, :]
+
+    if late is not None:
+        send_late_x.arrive()
+        gather_late = Exchange("exp", m, lambda p: xg.at[mine], lambda s: xg.at[s], *pair())
+        gather_late.start()
+    for h in range(nc):
+        gather_cot[h].arrive()
+    gather_mixed = []
+    for h in direct:
+        gather_mixed.append(
             Exchange("exp", m, lambda p, h=h: mx.at[h, mine], lambda s, h=h: mx.at[h, s], *pair())
         )
-        gather_x[h].start()
-
-    send_dy, send_x = [], []
-    for h in range(nc):
-        gather_cot[h].arrive()
+        gather_mixed[h].start()
+    send_dy = []
+    for h in range(nc):
         for k, part in enumerate(spread(pt[...], [cots[h, k] for k in range(m)])):
             sdy[h, :, spans(h, k)] = (part * gs[:, :cw]).astype(BF16)
         send_dy.append(Exchange("ctx", n, rows(sdy, h), rows(rdy, h), *pair()))
@@ -262,16 +278,14 @@
     share.arrive()
     total = jnp.sum(side[...], axis=0)[:1, :tokens]
     sc[...] = column(lax.rsqrt(total / width + EPS))
-    for h in range(nc):
-        gather_x[h].arrive()
-        normed = [
-            (mx[h, k].astype(F32) * side[k, 1 + h : 2 + h, :cw] * sc[:, :cw]).astype(BF16) for k in range(m)
-        ]
-        for k, part in enumerate(spread(pt[...], normed)):
+    send_x = []
+    for h in direct:
+        gather_mixed[h].arrive()
+        for k, part in enumerate(spread(pt[...], [mx[h, k] for k in range(m)])):
             sx[h, :, spans(h, k)] = part.astype(BF16)
-        send_x.append(Exchange("ctx", n, rows(sx, h), rows(rx, h), *pair()))
+        send_x.append(Exchange("ctx", n, rows(sx, h), rows(xa, h), *pair()))
         send_x[h].start()
-        rx[h, own, :] = sx[h, own, :]
+        xa[h, own, :] = sx[h, own, :]
 
     tile = min(256, inner)
     tiles = [slice(f, f + tile) for f in range(0, inner, tile)]
@@ -283,27 +297,40 @@
         dh[:, f] = dot(d_y, wd[f, :], LAST)
     weights[1].wait()
     weights[2].wait()
-    for h in range(nc):
+    for h in direct:
         send_x[h].arrive()
-        for f in tiles:
-            g = dot(rx[h], chan_rows(wg, h, f))
-            u = dot(rx[h], chan_rows(wu, h, f))
-            ga[:, f] = g if h == 0 else ga[:, f] + g
-            ua[:, f] = u if h == 0 else ua[:, f] + u
-            if h == nc - 1:
-                step = 32
-                for r in range(0, slots, step):
-                    at = slice(r, r + step)
-                    g, u, d = ga[at, f], ua[at, f], dh[at, f]
-                    sigma = jax.nn.sigmoid(g)
-                    swish = g * sigma
-                    hid[at, f] = (swish * u).astype(BF16)
-                    dg[at, f] = (d * u * sigma * (1.0 + g * (1.0 - sigma))).astype(BF16)
-                    du[at, f] = (d * swish).astype(BF16)
+    if late is not None:
+        gather_late.arrive()
+
+    def raw(k, h, at):
+        return (xg[k, at, :] if h == late else xa[h, at, spans(h, k)]).astype(F32)
+
+    step = 32
+    for r in range(0, slots, step):
+        at = slice(r, r + step)
+        acc = jnp.zeros((step, cw), F32)
+        for k in range(m):
+            for h in range(nc):
+                acc = acc + raw(k, h, at) * raw(k, h, at)
+        unit = lax.rsqrt(jnp.sum(acc, axis=1, keepdims=True) / width + EPS)
+        for k in range(m):
+            for h in range(nc):
+                lo = k * chans + h * cw
+                rx[at, lo : lo + cw] = (raw(k, h, at) * gain_of(k, h) * unit).astype(BF16)
+    for f in tiles:
+        ga[:, f] = dot(rx[...], wg[:, f])
+        ua[:, f] = dot(rx[...], wu[:, f])
+        for r in range(0, slots, step):
+            at = slice(r, r + step)
+            g, u, d = ga[at, f], ua[at, f], dh[at, f]
+            sigma = jax.nn.sigmoid(g)
+            swish = g * sigma
+            hid[at, f] = (swish * u).astype(BF16)
+            dg[at, f] = (d * u * sigma * (1.0 + g * (1.0 - sigma))).astype(BF16)
+            du[at, f] = (d * swish).astype(BF16)
 
     group = max(1, min(m, 256 // cw))
-    send_dx, send_y = [], []
-    for h in range(nc):
+    def row_grads(h):
         for k in range(0, m, group):
             if nc == 1:
                 at = slice(k * cw, (k + group) * cw)
@@ -315,11 +342,38 @@
                     )
                     for w in (wg, wu)
                 ]
-            part = dot(dg[...], w1, LAST) + dot(du[...], w2, LAST)
+            yield k, dot(dg[...], w1, LAST) + dot(du[...], w2, LAST)
+
+    send_dx, send_y = [], []
+    if late is not None:
+        inner_q = jnp.zeros((slots, cw), F32)
+        for k, part in row_grads(late):
+            for j in range(k, k + group):
+                piece = part[:, (j - k) * cw : (j - k + 1) * cw]
+                sl[j] = piece.astype(BF16)
+                inner_q = inner_q + piece * xg[j].astype(F32) * gain_of(j, late)
+        reduce_late = Exchange("exp", m, lambda p: sl.at[p], lambda s: rl.at[s], *pair())
+        reduce_late.start()
+        rl[mine] = sl[mine]
+        inner_q = jnp.sum(inner_q, axis=1, keepdims=True)
+        high = inner_q.astype(BF16).astype(F32)
+        lane = lax.broadcasted_iota(jnp.int32, (slots, 128), 1)
+        sdx[0, :, span_all:] = jnp.where(
+            lane == 0, high, jnp.where(lane == 1, inner_q - high, 0.0)
+        ).astype(BF16)
+    for h in direct:
+        for k, part in row_grads(h):
             sdx[h, :, k * cw : (k + group) * cw] = part.astype(BF16)
         send_dx.append(Exchange("ctx", n, rows(sdx, h), rows(bdx, h), *pair()))
         send_dx[h].start()
         bdx[h, own, :] = sdx[h, own, :]
+    for f in tiles:
+        gwd_ref[f, :] = dot(hid[:, f], natural(rdy, 0, width), FIRST).astype(BF16)
+    for lo in range(0, width, 256):
+        part = rx[:, lo : lo + 256]
+        gwg_ref[lo : lo + 256, :] = dot(part, dg[...], FIRST).astype(BF16)
+        gwu_ref[lo : lo + 256, :] = dot(part, du[...], FIRST).astype(BF16)
+
     for h in range(nc):
         for k in range(0, m, group):
             if nc == 1:
@@ -333,32 +387,35 @@
         send_y[h].start()
         by[h, own, :] = sy[h, own, :]
 
-    for f in tiles:
-        gwd_ref[f, :] = dot(hid[:, f], natural(rdy, 0, width), FIRST).astype(BF16)
-    for lo in range(0, width, 256):
-        part = natural(rx, lo, lo + 256)
-        gwg_ref[lo : lo + 256, :] = dot(part, dg[...], FIRST).astype(BF16)
-        gwu_ref[lo : lo + 256, :] = dot(part, du[...], FIRST).astype(BF16)
-
     sum_dx, sum_y = [], []
     weighted = jnp.zeros((tokens, cw), F32)
     sum_norm = Exchange("exp", m, lambda p: norm.at[mine], lambda s: norm.at[s], *pair())
-    for h in range(nc):
+    for h in direct:
         send_dx[h].arrive()
         full = dot(pb[...], bdx[h])
+        if h == 0 and late is not None:
+            late_q = full[:, span_all : span_all + 1] + full[:, span_all + 1 : span_all + 2]
         for k in range(m):
             part = full[:, spans(h, k)]
             zdx[h, k] = part.astype(BF16)
-            weighted = weighted + part * mx[h, k].astype(F32) * side[k, 1 + h : 2 + h, :cw]
-        if h == nc - 1:
-            row = turn_row(jnp.sum(weighted, axis=1, keepdims=True))
-            norm[mine] = jnp.broadcast_to(row, norm.shape[1:])
+            weighted = weighted + part * mx[h, k].astype(F32) * gain_of(k, h)
+        if h == direct[-1]:
+            total_q = jnp.sum(weighted, axis=1, keepdims=True)
+            if late is not None:
+                total_q = total_q + late_q
+            norm[mine] = jnp.broadcast_to(turn_row(total_q), norm.shape[1:])
             sum_norm.start()
         sum_dx.append(
             Exchange("exp", m, lambda p, h=h: zdx.at[h, p], lambda s, h=h: rdx.at[h, s], *pair())
         )
         sum_dx[h].start()
         rdx[h, mine] = zdx[h, mine]
+    if late is not None:
+        reduce_late.arrive()
+        ol[...] = jnp.sum(rl[...].astype(F32), axis=0).astype(BF16)
+        send_late = Exchange("ctx", n, rows(ol), rows(bl), *pair())
+        send_late.start()
+        bl[own, :] = ol[own, :]
 
     d0 = jnp.zeros((tokens, cw), F32)
     d1 = jnp.zeros((tokens, cw), F32)
@@ -378,18 +435,19 @@
         ry[h, mine] = zy[h, mine]
         return d0, d1
 
-    for h in range(nc - 1):
+    for h in range(nc):
         d0, d1 = combine(h, d0, d1)
-
-    for h in range(nc):
+    for h in direct:
         sum_dx[h].arrive()
     sum_norm.arrive()
+    if late is not None:
+        send_late.arrive()
     q = column(jnp.sum(norm[...], axis=0)[:1])
     scale = sc[...]
     pull = q * scale * scale * scale / width
     for h in range(nc):
         lanes = slice(h * cw, (h + 1) * cw)
-        dn = jnp.sum(rdx[h].astype(F32), axis=0)
+        dn = dot(pb[...], bl[...]) if h == late else jnp.sum(rdx[h].astype(F32), axis=0)
         mixed = mx[h, mine].astype(F32)
         dm = cots[h, mine].astype(F32) + gain_row[:, lanes] * dn * scale[:, :cw] - mixed * pull[:, :cw]
         dmp[EDGE : EDGE + tokens, lanes] = dm
@@ -400,12 +458,6 @@
         ).astype(BF16)
     halo_d = Halo(n, de, dl, dr, hs2)
     halo_d.start()
-    d0, d1 = combine(nc - 1, d0, d1)
-    dots[mine, 0:1, :] = turn_row(jnp.sum(d0, axis=1, keepdims=True))
-    dots[mine, 1:2, :] = turn_row(jnp.sum(d1, axis=1, keepdims=True))
-    sum_dots = Exchange("exp", m, lambda p: dots.at[mine], lambda s: dots.at[s], *pair())
-    sum_dots.start()
-
     for h in range(nc):
         lanes = slice(h * cw, (h + 1) * cw)
         dm = dmp[EDGE : EDGE + tokens, lanes]
@@ -416,6 +468,11 @@
             tp[me, j : j + 1, lanes] = term.astype(BF16)
     sum_taps = Exchange("ctx", n, lambda p: tp.at[me], lambda s: tp.at[s], *pair())
     sum_taps.start()
+    dots[mine, 0:1, :] = turn_row(jnp.sum(d0, axis=1, keepdims=True))
+    dots[mine, 1:2, :] = turn_row(jnp.sum(d1, axis=1, keepdims=True))
+    sum_dots = Exchange("exp", m, lambda p: dots.at[mine], lambda s: dots.at[s], *pair())
+    sum_dots.start()
+
     halo_d.arrive()
     dmp[:EDGE, :] = dl[...].astype(F32)
     dmp[EDGE + tokens :, :] = dr[...].astype(F32)
@@ -439,9 +496,10 @@
     grads = jnp.sum(tp[...].astype(F32), axis=0)
     tapo_ref[...] = grads[:taps]
     gaino_ref[...] = grads[taps : taps + 1]
-    for done in (halo, halo_d, share, sum_norm, sum_dots, sum_taps):
-        done.sent()
-    for group in (gather_cot, gather_x, send_dy, send_x, send_dx, send_y, sum_dx, sum_y):
+    singles = [halo, halo_d, share, sum_norm, sum_dots, sum_taps]
+    if late is not None:
+        singles += [reduce_late, send_late, send_late_x, gather_late]
+    for group in (singles, gather_cot, gather_mixed, send_x, send_dy, send_dx, send_y, sum_dx, sum_y):
         for done in group:
             done.sent()
 
@@ -469,7 +527,7 @@
     nc = max(1, chans // 128)
     cw = chans // nc
     vmem = pl.BlockSpec(memory_space=pltpu.VMEM)
-    hbm = pl.BlockSpec(memory_space=pl.ANY)
+    hbm = pl.BlockSpec(memory_space=pltpu.HBM)
     shape = jax.ShapeDtypeStruct
     dma = pltpu.SemaphoreType.DMA
     V = pltpu.VMEM
@@ -483,16 +541,27 @@
         shape((width, inner), BF16),
         shape((inner, width), BF16),
     )
-    sizes = [m] * nc + [m] + [m] * nc + [n] * (2 * nc) + [n] * (2 * nc) + [m]
-    sizes += [m] * nc + [m] * nc + [m] + [n]
+    straight = nc - 1 if nc > 1 else 1
+    extra = nc > 1
+    sizes = [m] * nc + [m] + [n, m] * extra + [m] * straight + [n] * nc + [n] * straight
+    sizes += [m] * extra + [n] * straight + [n] * nc + [m] + [m] * straight + [n] * extra
+    sizes += [m] * nc + [n] + [m]
     big = V((nc, slots, m * cw), BF16)
+    part = V((straight, slots, m * cw), BF16)
+    plus = V((straight, slots, m * cw + 128 * extra), BF16)
+    operands = [
+        pltpu.with_memory_space_constraint(a, pltpu.HBM)
+        for a in (
+            inputs, conv_taps.T, norm_gain, routes.T, gate_probs.T, grad_out, w_gate, w_up, w_down
+        )
+    ]
     results = pl.pallas_call(
         functools.partial(layer, n, m, taps, cap, nc),
         out_shape=outs,
         in_specs=[hbm] * 9,
         out_specs=(vmem,) * 8,
         scratch_shapes=[
-            V((chans, tokens), BF16), V((taps, chans), F32), V((1, chans), BF16),
+            V((chans, tokens), BF16), V((taps, chans), F32), V((chans,), BF16),
             V((2, tokens), jnp.int32), V((2, tokens), F32), V((chans, tokens), BF16),
             V((width, inner), BF16), V((width, inner), BF16), V((inner, width), BF16),
             V((tokens + 2 * EDGE, chans), F32), V((8, tokens + 24, chans), F32),
@@ -502,10 +571,11 @@
             V((slots, tokens), BF16), V((tokens, slots), BF16), V((tokens, slots), BF16),
             V((tokens, slots), BF16),
             V((slots, 128), F32), V((2, tokens, 128), F32), V((tokens, 128), F32),
-            big, big, big, big,
+            big, part, big, V((slots, width), BF16), V((slots, cw), BF16), part, V((m, slots, cw), BF16),
             V((slots, inner), F32), V((slots, inner), F32), V((slots, inner), F32),
             V((slots, inner), BF16), V((slots, inner), BF16), V((slots, inner), BF16),
-            big, big, big, big,
+            plus, big, plus, big,
+            V((m, slots, cw), BF16), V((m, slots, cw), BF16), V((slots, cw), BF16), V((slots, cw), BF16),
             V((nc, m, tokens, cw), BF16), V((nc, m, tokens, cw), BF16),
             V((nc, m, tokens, cw), BF16), V((nc, m, tokens, cw), BF16),
             V((m, 8, tokens), F32), V((m, 8, tokens), F32),
@@ -516,10 +586,13 @@
             *[dma((s,)) for s in sizes for _ in range(2)],
         ],
         compiler_params=pltpu.CompilerParams(
-            collective_id=0, has_side_effects=True, vmem_limit_bytes=48 << 20
+            collective_id=0, has_side_effects=True, vmem_limit_bytes=36 << 20
+        ),
+        cost_estimate=pl.CostEstimate(
+            flops=18 * slots * width * inner, bytes_accessed=12 * width * inner, transcendentals=slots * inner
         ),
         name="layer",
-    )(inputs, conv_taps.T, norm_gain[None], routes.T, gate_probs.T, grad_out, w_gate, w_up, w_down)
+    )(*operands)
     results = pl.pallas_call(
         finish,
         out_shape=outs,

time: 62 us -> 53.2 us (0.86)
  local copies, waits for them, and re-layouts: 6.04 us -> 0 us
  Pallas kernels: 55 us -> 52.4 us
    unnamed x12 -> x0, local copies, waits for them, and re-layouts: 5.38 us -> none
    pallas_call x1, Pallas kernels: 52.2 us -> 49.6 us  [local(): pl.pallas_call(functools.partial(layer, n, m, taps, cap, nc), out_shape=o...]
    broadcast_in_dim x1 -> x0, local copies, waits for them, and re-layouts: 0.66 us -> none  [local(): norm_gain[None]]
where the time goes in v2:
time: 53.2 us; the launch traced here: 53.1 us
  Pallas kernels  52.4 us (98%)
  between operations  0.64 us (1%)
    pallas_call x1, Pallas kernels, local(): pl.pallas_call(functools.partial(layer, n, m, taps, cap, nc), out_shape=o...  49.6 us
    pallas_call x1, Pallas kernels, local(): pl.pallas_call(finish, out_shape=outs, in_specs=[vmem] * 8, out_specs=(hb...  2.83 us

profile of v2, /device:TPU:0, one launch (start us, length us, event | category | flops | bytes accessed | tf_op | source)
XLA Modules:
  0.0 53.1 jit_solution(4889449774347475813)
XLA Ops:
  0.6 49.6 %layer.1 = (bf16[256,128]{1,0:T(8,128)(2,1)S(1)}, bf16[256,128]{1,0:T(8,128)(2,1)S(1)}, f32[31,256]{1,0:T(8,128)S(1)}, f32[1,256]{1,0:T(1,128)S(1)}, f32[2,128]{...) custom-call(bf16[256,128]{1,0:T(8,128)(2,1)} %x_any.1, ...), custom_call_target="tpu_custom_call" | custom-call | flops 4831838208 | bytes 12582912 | tf_op jit(solution)/shard_map/layer/pallas_call | solution.py:558
  50.2 2.8 %finish.1 = (bf16[256,128]{1,0:T(8,128)(2,1)}, bf16[256,128]{1,0:T(8,128)(2,1)}, f32[31,256]{1,0:T(8,128)}, f32[1,256]{1,0:T(1,128)}, f32[2,128]{1,0:T(2,128)}, ...) custom-call(bf16[256,128]{1,0:T(8,128)(2,1)S(1)} %get-tuple-element.24.refs_0_, ...), custom_call_target="tpu_custom_call" | custom-call | tf_op jit(solution)/shard_map/finish/pallas_call | solution.py:596

commit v3 on v2

--- a/solution.py
+++ b/solution.py
@@ -36,42 +36,42 @@
 
 
 class Exchange:
-    def __init__(self, axis, size, src, dst, send, recv):
+    def __init__(self, axis, size, src, dst, bulk, send, recv):
         self.axis, self.size, self.src, self.dst = axis, size, src, dst
-        self.send, self.recv = send, recv
+        self.bulk, self.send, self.recv = bulk, send, recv
         self.me = lax.axis_index(axis)
 
-    def copy(self, k, slot):
-        peer = lax.rem(self.me + k, self.size)
+    def where(self, peer):
         if self.axis == "ctx":
-            where = (peer, lax.axis_index("exp"))
-        else:
-            where = (lax.axis_index("ctx"), peer)
-        slot = peer if slot is None else slot
+            return peer, lax.axis_index("exp")
+        return lax.axis_index("ctx"), peer
+
+    def copy(self, peer, src, dst):
         return pltpu.make_async_remote_copy(
-            src_ref=self.src(peer),
-            dst_ref=self.dst(slot),
-            send_sem=self.send.at[peer],
-            recv_sem=self.recv.at[slot],
-            device_id=where,
+            src_ref=src,
+            dst_ref=dst,
+            send_sem=self.send,
+            recv_sem=self.recv,
+            device_id=self.where(peer),
             device_id_type=MESH,
         )
 
-    def each(self, act):
+    def start(self):
         def body(k, _):
-            act(k)
+            peer = lax.rem(self.me + k, self.size)
+            self.copy(peer, self.src(peer), self.dst(self.me)).start()
             return 0
 
         lax.fori_loop(1, self.size, body, 0)
 
-    def start(self):
-        self.each(lambda k: self.copy(k, self.me).start())
+    def all_of_them(self):
+        return self.copy(lax.rem(self.me + 1, self.size), self.bulk, self.bulk)
 
     def arrive(self):
-        self.each(lambda k: self.copy(k, None).wait_recv())
+        self.all_of_them().wait_recv()
 
     def sent(self):
-        self.each(lambda k: self.copy(k, self.me).wait_send())
+        self.all_of_them().wait_send()
 
 
 class Halo:
@@ -120,30 +120,24 @@
           xp, xs, xe, hl, hr, cots, mx, side, pt, pb, p0s, p1s, gs, gc, sc,
           sdy, sx, rdy, rx, sxl, xa, xg, dh, ga, ua, hid, dg, du, sdx, sy, bdx, by, sl, rl, ol, bl,
           zdx, zy, rdx, ry, dots, norm, dmp, de, dl, dr, tp,
-          lsem, hs, hs2, *sem):
+          lsem, hs, hs2, sem):
     me, mine = lax.axis_index("ctx"), lax.axis_index("exp")
     chans, tokens = x_s.shape
     slots = pt.shape[0]
     width, inner = wg.shape
     cw = chans // nc
-    it = iter(sem)
+    it = iter(range(sem.shape[0]))
     own = pl.ds(pl.multiple_of(me * cap, cap), cap)
+    most = (n - 1) * cap
     late = nc - 1 if nc > 1 else None
     direct = [h for h in range(nc) if h != late]
     span_all = m * cw
 
     def pair():
-        return next(it), next(it)
+        return sem.at[next(it)], sem.at[next(it)]
 
     def spans(h, k):
         return slice(k * cw, (k + 1) * cw)
-
-    def chan_rows(ref, h, cols=slice(None)):
-        if nc == 1:
-            return ref[:, cols]
-        return jnp.concatenate(
-            [ref[k * chans + h * cw : k * chans + (h + 1) * cw, cols] for k in range(m)], axis=0
-        )
 
     def natural(ref, lo, hi):
         if nc == 1:
@@ -196,8 +190,9 @@
     gather_cot = []
     for h in range(nc):
         gather_cot.append(
-            Exchange("exp", m, lambda p, h=h: cots.at[h, mine], lambda s, h=h: cots.at[h, s], *pair())
-        )
+            Exchange("exp", m, lambda p, h=h: cots.at[h, mine], lambda s, h=h: cots.at[h, s], cots.at[h, :m - 1], *pair())
+        )
+    for h in range(nc):
         gather_cot[h].start()
 
     for load in loads[2:]:
@@ -248,33 +243,39 @@
         squares = squares + jnp.sum(mixed * mixed, axis=1, keepdims=True)
         side[mine, 1 + h : 2 + h, :cw] = gain_row[:, lanes]
     side[mine, 0:1, :tokens] = turn_row(squares)
-    share = Exchange("exp", m, lambda p: side.at[mine], lambda s: side.at[s], *pair())
+    share = Exchange("exp", m, lambda p: side.at[mine], lambda s: side.at[s], side.at[:m - 1], *pair())
     share.start()
     if late is not None:
         sxl[...] = dot(pt[...], mx[late, mine]).astype(BF16)
-        send_late_x = Exchange("ctx", n, rows(sxl), rows(xg, mine), *pair())
-        send_late_x.start()
+        launch_x = Exchange("ctx", n, rows(sxl), rows(xg, mine), xg.at[mine, :most], *pair())
+        launch_x.start()
         xg[mine, own, :] = sxl[own, :]
 
-    if late is not None:
-        send_late_x.arrive()
-        gather_late = Exchange("exp", m, lambda p: xg.at[mine], lambda s: xg.at[s], *pair())
-        gather_late.start()
-    for h in range(nc):
-        gather_cot[h].arrive()
     gather_mixed = []
     for h in direct:
         gather_mixed.append(
-            Exchange("exp", m, lambda p, h=h: mx.at[h, mine], lambda s, h=h: mx.at[h, s], *pair())
+            Exchange("exp", m, lambda p, h=h: mx.at[h, mine], lambda s, h=h: mx.at[h, s], mx.at[h, :m - 1], *pair())
         )
         gather_mixed[h].start()
+
     send_dy = []
-    for h in range(nc):
+
+    def dispatch_cot(h):
+        gather_cot[h].arrive()
         for k, part in enumerate(spread(pt[...], [cots[h, k] for k in range(m)])):
             sdy[h, :, spans(h, k)] = (part * gs[:, :cw]).astype(BF16)
-        send_dy.append(Exchange("ctx", n, rows(sdy, h), rows(rdy, h), *pair()))
+        send_dy.append(Exchange("ctx", n, rows(sdy, h), rows(rdy, h), rdy.at[h, :most], *pair()))
         send_dy[h].start()
         rdy[h, own, :] = sdy[h, own, :]
+
+    if late is not None:
+        gather_late = Exchange("exp", m, lambda p: xg.at[mine], lambda s: xg.at[s], xg.at[:m - 1], *pair())
+    dispatch_cot(0)
+    if late is not None:
+        launch_x.arrive()
+        gather_late.start()
+    for h in range(1, nc):
+        dispatch_cot(h)
     share.arrive()
     total = jnp.sum(side[...], axis=0)[:1, :tokens]
     sc[...] = column(lax.rsqrt(total / width + EPS))
@@ -283,7 +284,7 @@
         gather_mixed[h].arrive()
         for k, part in enumerate(spread(pt[...], [mx[h, k] for k in range(m)])):
             sx[h, :, spans(h, k)] = part.astype(BF16)
-        send_x.append(Exchange("ctx", n, rows(sx, h), rows(xa, h), *pair()))
+        send_x.append(Exchange("ctx", n, rows(sx, h), rows(xa, h), xa.at[h, :most], *pair()))
         send_x[h].start()
         xa[h, own, :] = sx[h, own, :]
 
@@ -351,8 +352,8 @@
             for j in range(k, k + group):
                 piece = part[:, (j - k) * cw : (j - k + 1) * cw]
                 sl[j] = piece.astype(BF16)
-                inner_q = inner_q + piece * xg[j].astype(F32) * gain_of(j, late)
-        reduce_late = Exchange("exp", m, lambda p: sl.at[p], lambda s: rl.at[s], *pair())
+                inner_q = inner_q + piece * raw(j, late, slice(None)) * gain_of(j, late)
+        reduce_late = Exchange("exp", m, lambda p: sl.at[p], lambda s: rl.at[s], rl.at[:m - 1], *pair())
         reduce_late.start()
         rl[mine] = sl[mine]
         inner_q = jnp.sum(inner_q, axis=1, keepdims=True)
@@ -364,16 +365,9 @@
     for h in direct:
         for k, part in row_grads(h):
             sdx[h, :, k * cw : (k + group) * cw] = part.astype(BF16)
-        send_dx.append(Exchange("ctx", n, rows(sdx, h), rows(bdx, h), *pair()))
+        send_dx.append(Exchange("ctx", n, rows(sdx, h), rows(bdx, h), bdx.at[h, :most], *pair()))
         send_dx[h].start()
         bdx[h, own, :] = sdx[h, own, :]
-    for f in tiles:
-        gwd_ref[f, :] = dot(hid[:, f], natural(rdy, 0, width), FIRST).astype(BF16)
-    for lo in range(0, width, 256):
-        part = rx[:, lo : lo + 256]
-        gwg_ref[lo : lo + 256, :] = dot(part, dg[...], FIRST).astype(BF16)
-        gwu_ref[lo : lo + 256, :] = dot(part, du[...], FIRST).astype(BF16)
-
     for h in range(nc):
         for k in range(0, m, group):
             if nc == 1:
@@ -383,13 +377,20 @@
                     [wd[:, j * chans + h * cw : j * chans + (h + 1) * cw] for j in range(k, k + group)], axis=1
                 )
             sy[h, :, k * cw : (k + group) * cw] = dot(hid[...], w).astype(BF16)
-        send_y.append(Exchange("ctx", n, rows(sy, h), rows(by, h), *pair()))
+        send_y.append(Exchange("ctx", n, rows(sy, h), rows(by, h), by.at[h, :most], *pair()))
         send_y[h].start()
         by[h, own, :] = sy[h, own, :]
 
+    for f in tiles:
+        gwd_ref[f, :] = dot(hid[:, f], natural(rdy, 0, width), FIRST).astype(BF16)
+    for lo in range(0, width, 256):
+        part = rx[:, lo : lo + 256]
+        gwg_ref[lo : lo + 256, :] = dot(part, dg[...], FIRST).astype(BF16)
+        gwu_ref[lo : lo + 256, :] = dot(part, du[...], FIRST).astype(BF16)
+
     sum_dx, sum_y = [], []
     weighted = jnp.zeros((tokens, cw), F32)
-    sum_norm = Exchange("exp", m, lambda p: norm.at[mine], lambda s: norm.at[s], *pair())
+    sum_norm = Exchange("exp", m, lambda p: norm.at[mine], lambda s: norm.at[s], norm.at[:m - 1], *pair())
     for h in direct:
         send_dx[h].arrive()
         full = dot(pb[...], bdx[h])
@@ -406,14 +407,14 @@
             norm[mine] = jnp.broadcast_to(turn_row(total_q), norm.shape[1:])
             sum_norm.start()
         sum_dx.append(
-            Exchange("exp", m, lambda p, h=h: zdx.at[h, p], lambda s, h=h: rdx.at[h, s], *pair())
+            Exchange("exp", m, lambda p, h=h: zdx.at[h, p], lambda s, h=h: rdx.at[h, s], rdx.at[h, :m - 1], *pair())
         )
         sum_dx[h].start()
         rdx[h, mine] = zdx[h, mine]
     if late is not None:
         reduce_late.arrive()
         ol[...] = jnp.sum(rl[...].astype(F32), axis=0).astype(BF16)
-        send_late = Exchange("ctx", n, rows(ol), rows(bl), *pair())
+        send_late = Exchange("ctx", n, rows(ol), rows(bl), bl.at[:most], *pair())
         send_late.start()
         bl[own, :] = ol[own, :]
 
@@ -429,7 +430,7 @@
             cot = cots[h, k].astype(F32)
             d0, d1 = d0 + a * cot, d1 + b * cot
         sum_y.append(
-            Exchange("exp", m, lambda p, h=h: zy.at[h, p], lambda s, h=h: ry.at[h, s], *pair())
+            Exchange("exp", m, lambda p, h=h: zy.at[h, p], lambda s, h=h: ry.at[h, s], ry.at[h, :m - 1], *pair())
         )
         sum_y[h].start()
         ry[h, mine] = zy[h, mine]
@@ -466,11 +467,11 @@
             b = o % 8
             term = jnp.sum(dm * xs[b, o - b : o - b + tokens, lanes], axis=0, keepdims=True)
             tp[me, j : j + 1, lanes] = term.astype(BF16)
-    sum_taps = Exchange("ctx", n, lambda p: tp.at[me], lambda s: tp.at[s], *pair())
+    sum_taps = Exchange("ctx", n, lambda p: tp.at[me], lambda s: tp.at[s], tp.at[:n - 1], *pair())
     sum_taps.start()
     dots[mine, 0:1, :] = turn_row(jnp.sum(d0, axis=1, keepdims=True))
     dots[mine, 1:2, :] = turn_row(jnp.sum(d1, axis=1, keepdims=True))
-    sum_dots = Exchange("exp", m, lambda p: dots.at[mine], lambda s: dots.at[s], *pair())
+    sum_dots = Exchange("exp", m, lambda p: dots.at[mine], lambda s: dots.at[s], dots.at[:m - 1], *pair())
     sum_dots.start()
 
     halo_d.arrive()
@@ -498,7 +499,7 @@
     gaino_ref[...] = grads[taps : taps + 1]
     singles = [halo, halo_d, share, sum_norm, sum_dots, sum_taps]
     if late is not None:
-        singles += [reduce_late, send_late, send_late_x, gather_late]
+        singles += [reduce_late, send_late, launch_x, gather_late]
     for group in (singles, gather_cot, gather_mixed, send_x, send_dy, send_dx, send_y, sum_dx, sum_y):
         for done in group:
             done.sent()
@@ -524,7 +525,7 @@
     cap = max(tokens // 8, (2 * tokens + n - 1) // n)
     slots = n * cap
     pad = -(-(taps + 1) // 16) * 16
-    nc = max(1, chans // 128)
+    nc = 2 if chans % 256 == 0 else 1
     cw = chans // nc
     vmem = pl.BlockSpec(memory_space=pltpu.VMEM)
     hbm = pl.BlockSpec(memory_space=pltpu.HBM)
@@ -543,11 +544,8 @@
     )
     straight = nc - 1 if nc > 1 else 1
     extra = nc > 1
-    sizes = [m] * nc + [m] + [n, m] * extra + [m] * straight + [n] * nc + [n] * straight
-    sizes += [m] * extra + [n] * straight + [n] * nc + [m] + [m] * straight + [n] * extra
-    sizes += [m] * nc + [n] + [m]
     big = V((nc, slots, m * cw), BF16)
-    part = V((straight, slots, m * cw), BF16)
+    part = V((nc, slots, m * cw), BF16)
     plus = V((straight, slots, m * cw + 128 * extra), BF16)
     operands = [
         pltpu.with_memory_space_constraint(a, pltpu.HBM)
@@ -583,7 +581,7 @@
             V((2, EDGE, chans), BF16), V((EDGE, chans), BF16), V((EDGE, chans), BF16),
             V((n, pad, chans), BF16),
             dma((9,)), dma((4,)), dma((4,)),
-            *[dma((s,)) for s in sizes for _ in range(2)],
+            dma((64,)),
         ],
         compiler_params=pltpu.CompilerParams(
             collective_id=0, has_side_effects=True, vmem_limit_bytes=36 << 20

time: 53.2 us -> 47.8 us (0.90)
  Pallas kernels: 52.4 us -> 47 us
    pallas_call x1, Pallas kernels: 49.6 us -> 44.2 us  [local(): pl.pallas_call(functools.partial(layer, n, m, taps, cap, nc), out_shape=o...]
where the time goes in v3:
time: 47.8 us; the launch traced here: 47.7 us
  Pallas kernels  47 us (98%)
  between operations  0.64 us (1%)
    pallas_call x1, Pallas kernels, local(): pl.pallas_call(functools.partial(layer, n, m, taps, cap, nc), out_shape=o...  44.2 us
    pallas_call x1, Pallas kernels, local(): pl.pallas_call(finish, out_shape=outs, in_specs=[vmem] * 8, out_specs=(hb...  2.83 us

profile of v3, /device:TPU:0, one launch (start us, length us, event | category | flops | bytes accessed | tf_op | source)
XLA Modules:
  0.0 47.7 jit_solution(8398918617464475982)
XLA Ops:
  0.6 44.2 %layer.1 = (bf16[256,128]{1,0:T(8,128)(2,1)S(1)}, bf16[256,128]{1,0:T(8,128)(2,1)S(1)}, f32[31,256]{1,0:T(8,128)S(1)}, f32[1,256]{1,0:T(1,128)S(1)}, f32[2,128]{...) custom-call(bf16[256,128]{1,0:T(8,128)(2,1)} %x_any.1, ...), custom_call_target="tpu_custom_call" | custom-call | flops 4831838208 | bytes 12582912 | tf_op jit(solution)/shard_map/layer/pallas_call | solution.py:556
  44.8 2.8 %finish.1 = (bf16[256,128]{1,0:T(8,128)(2,1)}, bf16[256,128]{1,0:T(8,128)(2,1)}, f32[31,256]{1,0:T(8,128)}, f32[1,256]{1,0:T(1,128)}, f32[2,128]{1,0:T(2,128)}, ...) custom-call(bf16[256,128]{1,0:T(8,128)(2,1)S(1)} %get-tuple-element.24.refs_0_, ...), custom_call_target="tpu_custom_call" | custom-call | tf_op jit(solution)/shard_map/finish/pallas_call | solution.py:594

commit v4 on v3

--- a/solution.py
+++ b/solution.py
@@ -118,7 +118,7 @@
           lo_ref, gin_ref, tapo_ref, gaino_ref, gateo_ref, gwg_ref, gwu_ref, gwd_ref,
           x_s, tap_s, gain_s, route_s, prob_s, cot_s, wg, wu, wd,
           xp, xs, xe, hl, hr, cots, mx, side, pt, pb, p0s, p1s, gs, gc, sc,
-          sdy, sx, rdy, rx, sxl, xa, xg, dh, ga, ua, hid, dg, du, sdx, sy, bdx, by, sl, rl, ol, bl,
+          sdy, sx, rdy, rx, sxl, xa, xg, gained, unit, dh, ga, ua, hid, dg, du, sdx, sy, bdx, by, sl, rl, ol, bl,
           zdx, zy, rdx, ry, dots, norm, dmp, de, dl, dr, tp,
           lsem, hs, hs2, sem):
     me, mine = lax.axis_index("ctx"), lax.axis_index("exp")
@@ -228,6 +228,16 @@
     xp[EDGE + tokens :, :] = hr[...].astype(F32)
     base = EDGE - taps // 2
     span = tokens + 24
+    gather_mixed = []
+
+    def begin_mixed():
+        for h in direct:
+            gather_mixed.append(
+                Exchange("exp", m, lambda p, h=h: mx.at[h, mine], lambda s, h=h: mx.at[h, s], mx.at[h, :m - 1], *pair())
+            )
+            gather_mixed[h].start()
+
+
     squares = jnp.zeros((tokens, 1), F32)
     for h in range(nc):
         lanes = slice(h * cw, (h + 1) * cw)
@@ -251,13 +261,7 @@
         launch_x.start()
         xg[mine, own, :] = sxl[own, :]
 
-    gather_mixed = []
-    for h in direct:
-        gather_mixed.append(
-            Exchange("exp", m, lambda p, h=h: mx.at[h, mine], lambda s, h=h: mx.at[h, s], mx.at[h, :m - 1], *pair())
-        )
-        gather_mixed[h].start()
-
+    begin_mixed()
     send_dy = []
 
     def dispatch_cot(h):
@@ -290,46 +294,64 @@
 
     tile = min(256, inner)
     tiles = [slice(f, f + tile) for f in range(0, inner, tile)]
+    step = 32
+
+    def raw(k, h, at):
+        return (xg[k, at, :] if h == late else xa[h, at, spans(h, k)]).astype(F32)
+
+    def weigh(h):
+        for r in range(0, slots, step):
+            at = slice(r, r + step)
+            acc = jnp.zeros((step, cw), F32)
+            for k in range(m):
+                part = raw(k, h, at)
+                acc = acc + part * part
+                gained[h, at, spans(h, k)] = (part * gain_of(k, h)).astype(BF16)
+            total = jnp.broadcast_to(jnp.sum(acc, axis=1, keepdims=True), (step, 128))
+            unit[at] = total if h == first else unit[at] + total
+
+    def chan_rows(ref, h, cols):
+        if nc == 1:
+            return ref[:, cols]
+        return jnp.concatenate(
+            [ref[k * chans + h * cw : k * chans + (h + 1) * cw, cols] for k in range(m)], axis=0
+        )
+
+    def project(h, f):
+        for ref, w in ((ga, wg), (ua, wu)):
+            part = dot(gained[h], chan_rows(w, h, f))
+            ref[:, f] = part if h == first else ref[:, f] + part
+
     weights[0].wait()
+    weights[1].wait()
+    weights[2].wait()
+    first = direct[0] if late is None else late
+    if late is not None:
+        gather_late.arrive()
+        weigh(late)
+        for f in tiles:
+            project(late, f)
     for h in range(nc):
         send_dy[h].arrive()
     d_y = natural(rdy, 0, width)
     for f in tiles:
         dh[:, f] = dot(d_y, wd[f, :], LAST)
-    weights[1].wait()
-    weights[2].wait()
     for h in direct:
         send_x[h].arrive()
-    if late is not None:
-        gather_late.arrive()
-
-    def raw(k, h, at):
-        return (xg[k, at, :] if h == late else xa[h, at, spans(h, k)]).astype(F32)
-
-    step = 32
-    for r in range(0, slots, step):
-        at = slice(r, r + step)
-        acc = jnp.zeros((step, cw), F32)
-        for k in range(m):
-            for h in range(nc):
-                acc = acc + raw(k, h, at) * raw(k, h, at)
-        unit = lax.rsqrt(jnp.sum(acc, axis=1, keepdims=True) / width + EPS)
-        for k in range(m):
-            for h in range(nc):
-                lo = k * chans + h * cw
-                rx[at, lo : lo + cw] = (raw(k, h, at) * gain_of(k, h) * unit).astype(BF16)
+        weigh(h)
+    unit[...] = lax.rsqrt(unit[...] / width + EPS)
     for f in tiles:
-        ga[:, f] = dot(rx[...], wg[:, f])
-        ua[:, f] = dot(rx[...], wu[:, f])
+        for h in direct:
+            project(h, f)
         for r in range(0, slots, step):
             at = slice(r, r + step)
-            g, u, d = ga[at, f], ua[at, f], dh[at, f]
+            each = jnp.concatenate([unit[at]] * (tile // 128), axis=1)
+            g, u, d = ga[at, f] * each, ua[at, f] * each, dh[at, f]
             sigma = jax.nn.sigmoid(g)
             swish = g * sigma
             hid[at, f] = (swish * u).astype(BF16)
             dg[at, f] = (d * u * sigma * (1.0 + g * (1.0 - sigma))).astype(BF16)
             du[at, f] = (d * swish).astype(BF16)
-
     group = max(1, min(m, 256 // cw))
     def row_grads(h):
         for k in range(0, m, group):
@@ -362,13 +384,14 @@
         sdx[0, :, span_all:] = jnp.where(
             lane == 0, high, jnp.where(lane == 1, inner_q - high, 0.0)
         ).astype(BF16)
-    for h in direct:
-        for k, part in row_grads(h):
-            sdx[h, :, k * cw : (k + group) * cw] = part.astype(BF16)
-        send_dx.append(Exchange("ctx", n, rows(sdx, h), rows(bdx, h), bdx.at[h, :most], *pair()))
-        send_dx[h].start()
-        bdx[h, own, :] = sdx[h, own, :]
-    for h in range(nc):
+    def act_dx():
+        for h in direct:
+            for k, part in row_grads(h):
+                sdx[h, :, k * cw : (k + group) * cw] = part.astype(BF16)
+            send_dx.append(Exchange("ctx", n, rows(sdx, h), rows(bdx, h), bdx.at[h, :most], *pair()))
+            send_dx[h].start()
+            bdx[h, own, :] = sdx[h, own, :]
+    def act_y(h):
         for k in range(0, m, group):
             if nc == 1:
                 w = wd[:, k * cw : (k + group) * cw]
@@ -381,12 +404,29 @@
         send_y[h].start()
         by[h, own, :] = sy[h, own, :]
 
-    for f in tiles:
-        gwd_ref[f, :] = dot(hid[:, f], natural(rdy, 0, width), FIRST).astype(BF16)
-    for lo in range(0, width, 256):
-        part = rx[:, lo : lo + 256]
-        gwg_ref[lo : lo + 256, :] = dot(part, dg[...], FIRST).astype(BF16)
-        gwu_ref[lo : lo + 256, :] = dot(part, du[...], FIRST).astype(BF16)
+    def act_grads(part):
+        if part == 0:
+            for f in tiles:
+                gwd_ref[f, :] = dot(hid[:, f], natural(rdy, 0, width), FIRST).astype(BF16)
+        if part == 1:
+            for r in range(0, slots, step):
+                at = slice(r, r + step)
+                for k in range(m):
+                    for h in range(nc):
+                        lo = k * chans + h * cw
+                        normed = raw(k, h, at) * gain_of(k, h) * unit[at, :cw]
+                        rx[at, lo : lo + cw] = normed.astype(BF16)
+            for lo in range(0, width, 256):
+                part = rx[:, lo : lo + 256]
+                gwg_ref[lo : lo + 256, :] = dot(part, dg[...], FIRST).astype(BF16)
+                gwu_ref[lo : lo + 256, :] = dot(part, du[...], FIRST).astype(BF16)
+
+    act_dx()
+    act_y(0)
+    act_grads(0)
+    act_grads(1)
+    for h in range(1, nc):
+        act_y(h)
 
     sum_dx, sum_y = [], []
     weighted = jnp.zeros((tokens, cw), F32)
@@ -411,16 +451,6 @@
         )
         sum_dx[h].start()
         rdx[h, mine] = zdx[h, mine]
-    if late is not None:
-        reduce_late.arrive()
-        ol[...] = jnp.sum(rl[...].astype(F32), axis=0).astype(BF16)
-        send_late = Exchange("ctx", n, rows(ol), rows(bl), bl.at[:most], *pair())
-        send_late.start()
-        bl[own, :] = ol[own, :]
-
-    d0 = jnp.zeros((tokens, cw), F32)
-    d1 = jnp.zeros((tokens, cw), F32)
-
     def combine(h, d0, d1):
         send_y[h].arrive()
         y0, y1 = dot(p0s[...], by[h]), dot(p1s[...], by[h])
@@ -435,6 +465,15 @@
         sum_y[h].start()
         ry[h, mine] = zy[h, mine]
         return d0, d1
+
+    d0 = jnp.zeros((tokens, cw), F32)
+    d1 = jnp.zeros((tokens, cw), F32)
+    if late is not None:
+        reduce_late.arrive()
+        ol[...] = jnp.sum(rl[...].astype(F32), axis=0).astype(BF16)
+        send_late = Exchange("ctx", n, rows(ol), rows(bl), bl.at[:most], *pair())
+        send_late.start()
+        bl[own, :] = ol[own, :]
 
     for h in range(nc):
         d0, d1 = combine(h, d0, d1)
@@ -487,16 +526,16 @@
                 j = EDGE + taps // 2 - o
                 acc = acc + tap_s[j : j + 1, lanes] * moved[o - b : o - b + tokens]
         gin_ref[lanes, :] = jnp.transpose(acc).astype(BF16)
+    sum_taps.arrive()
+    grads = jnp.sum(tp[...].astype(F32), axis=0)
+    tapo_ref[...] = grads[:taps]
+    gaino_ref[...] = grads[taps : taps + 1]
     for h in range(nc):
         sum_y[h].arrive()
         out = mx[h, mine].astype(F32) + jnp.sum(ry[h].astype(F32), axis=0)
         lo_ref[h * cw : (h + 1) * cw, :] = jnp.transpose(out).astype(BF16)
     sum_dots.arrive()
     gateo_ref[...] = jnp.sum(dots[...], axis=0)[:2]
-    sum_taps.arrive()
-    grads = jnp.sum(tp[...].astype(F32), axis=0)
-    tapo_ref[...] = grads[:taps]
-    gaino_ref[...] = grads[taps : taps + 1]
     singles = [halo, halo_d, share, sum_norm, sum_dots, sum_taps]
     if late is not None:
         singles += [reduce_late, send_late, launch_x, gather_late]
@@ -569,7 +608,7 @@
             V((slots, tokens), BF16), V((tokens, slots), BF16), V((tokens, slots), BF16),
             V((tokens, slots), BF16),
             V((slots, 128), F32), V((2, tokens, 128), F32), V((tokens, 128), F32),
-            big, part, big, V((slots, width), BF16), V((slots, cw), BF16), part, V((m, slots, cw), BF16),
+            big, part, big, V((slots, width), BF16), V((slots, cw), BF16), part, V((m, slots, cw), BF16), big, V((slots, 128), F32),
             V((slots, inner), F32), V((slots, inner), F32), V((slots, inner), F32),
             V((slots, inner), BF16), V((slots, inner), BF16), V((slots, inner), BF16),
             plus, big, plus, big,
@@ -581,7 +620,7 @@
             V((2, EDGE, chans), BF16), V((EDGE, chans), BF16), V((EDGE, chans), BF16),
             V((n, pad, chans), BF16),
             dma((9,)), dma((4,)), dma((4,)),
-            dma((64,)),
+            dma((42,)),
         ],
         compiler_params=pltpu.CompilerParams(
             collective_id=0, has_side_effects=True, vmem_limit_bytes=36 << 20

time: 47.8 us -> 47 us (0.983)
  Pallas kernels: 47 us -> 46.2 us
    pallas_call x1, Pallas kernels: 44.2 us -> 43.4 us  [local(): pl.pallas_call(functools.partial(layer, n, m, taps, cap, nc), out_shape=o...]
where the time goes in v4:
time: 47 us; the launch traced here: 46.9 us
  Pallas kernels  46.2 us (98%)
  between operations  0.64 us (1%)
    pallas_call x1, Pallas kernels, local(): pl.pallas_call(functools.partial(layer, n, m, taps, cap, nc), out_shape=o...  43.4 us
    pallas_call x1, Pallas kernels, local(): pl.pallas_call(finish, out_shape=outs, in_specs=[vmem] * 8, out_specs=(hb...  2.83 us

profile of v4, /device:TPU:0, one launch (start us, length us, event | category | flops | bytes accessed | tf_op | source)
XLA Modules:
  0.0 46.9 jit_solution(14953537689766990184)
XLA Ops:
  0.6 43.4 %layer.1 = (bf16[256,128]{1,0:T(8,128)(2,1)S(1)}, bf16[256,128]{1,0:T(8,128)(2,1)S(1)}, f32[31,256]{1,0:T(8,128)S(1)}, f32[1,256]{1,0:T(1,128)S(1)}, f32[2,128]{...) custom-call(bf16[256,128]{1,0:T(8,128)(2,1)} %x_any.1, ...), custom_call_target="tpu_custom_call" | custom-call | flops 4831838208 | bytes 12582912 | tf_op jit(solution)/shard_map/layer/pallas_call | solution.py:595
  44.1 2.8 %finish.1 = (bf16[256,128]{1,0:T(8,128)(2,1)}, bf16[256,128]{1,0:T(8,128)(2,1)}, f32[31,256]{1,0:T(8,128)}, f32[1,256]{1,0:T(1,128)}, f32[2,128]{1,0:T(2,128)}, ...) custom-call(bf16[256,128]{1,0:T(8,128)(2,1)S(1)} %get-tuple-element.24.refs_0_, ...), custom_call_target="tpu_custom_call" | custom-call | tf_op jit(solution)/shard_map/finish/pallas_call | solution.py:633

commit v5 on v4

--- a/solution.py
+++ b/solution.py
@@ -376,7 +376,6 @@
                 sl[j] = piece.astype(BF16)
                 inner_q = inner_q + piece * raw(j, late, slice(None)) * gain_of(j, late)
         reduce_late = Exchange("exp", m, lambda p: sl.at[p], lambda s: rl.at[s], rl.at[:m - 1], *pair())
-        reduce_late.start()
         rl[mine] = sl[mine]
         inner_q = jnp.sum(inner_q, axis=1, keepdims=True)
         high = inner_q.astype(BF16).astype(F32)
@@ -422,6 +421,8 @@
                 gwu_ref[lo : lo + 256, :] = dot(part, du[...], FIRST).astype(BF16)
 
     act_dx()
+    if late is not None:
+        reduce_late.start()
     act_y(0)
     act_grads(0)
     act_grads(1)

time: 47 us -> 46.8 us (level)
  no operation moved by 1% of the time
where the time goes in v5:
time: 46.8 us; the launch traced here: 46.7 us
  Pallas kernels  46 us (98%)
  between operations  0.64 us (1%)
    pallas_call x1, Pallas kernels, local(): pl.pallas_call(functools.partial(layer, n, m, taps, cap, nc), out_shape=o...  43.2 us
    pallas_call x1, Pallas kernels, local(): pl.pallas_call(finish, out_shape=outs, in_specs=[vmem] * 8, out_specs=(hb...  2.83 us

profile of v5, /device:TPU:0, one launch (start us, length us, event | category | flops | bytes accessed | tf_op | source)
XLA Modules:
  0.0 46.7 jit_solution(258740003693817258)
XLA Ops:
  0.6 43.2 %layer.1 = (bf16[256,128]{1,0:T(8,128)(2,1)S(1)}, bf16[256,128]{1,0:T(8,128)(2,1)S(1)}, f32[31,256]{1,0:T(8,128)S(1)}, f32[1,256]{1,0:T(1,128)S(1)}, f32[2,128]{...) custom-call(bf16[256,128]{1,0:T(8,128)(2,1)} %x_any.1, ...), custom_call_target="tpu_custom_call" | custom-call | flops 4831838208 | bytes 12582912 | tf_op jit(solution)/shard_map/layer/pallas_call | solution.py:596
  43.9 2.8 %finish.1 = (bf16[256,128]{1,0:T(8,128)(2,1)}, bf16[256,128]{1,0:T(8,128)(2,1)}, f32[31,256]{1,0:T(8,128)}, f32[1,256]{1,0:T(1,128)}, f32[2,128]{1,0:T(2,128)}, ...) custom-call(bf16[256,128]{1,0:T(8,128)(2,1)S(1)} %get-tuple-element.24.refs_0_, ...), custom_call_target="tpu_custom_call" | custom-call | tf_op jit(solution)/shard_map/finish/pallas_call | solution.py:634
